TPU v7x, 1024 devices: a whole 4x8x16 slice. The times are simulated.
1024 devices in a mesh: row: 8 (over z_hi, core), col: 128 (over z_lo, y, x).
Axes of the slice: x: 4, y: 8, z: 16 (z_hi: 4, z_lo: 4; z = z_hi * 4 + z_lo), core: 2. Of those that a mesh axis runs over, the one named last changes fastest.
Arguments:
- user_emb: bfloat16 [32768, 64], P(('row', 'col')), may hold values from -6 to 6
- item_emb: bfloat16 [65536, 64], P(('row', 'col')), may hold values from -6 to 6
- user_degree: int32 [32768], P(('row', 'col')), may hold values from 1 to 16
- item_degree: int32 [65536], P(('row', 'col')), may hold values from 1 to 16
- block_values: bfloat16 [8, 128, 8, 128, 128], P('row', 'col'), may hold values from 0 to 1, as said below
- block_row: int32 [8, 128, 8], P('row', 'col'), may hold values from 0 to 31, as said below
- block_col: int32 [8, 128, 8], P('row', 'col'), may hold values from 0 to 3, as said below
- block_count: int32 [8, 128], P('row', 'col'), may hold values from 1 to 8, as said below
Outputs:
- user_final: bfloat16 [32768, 64], P(('row', 'col'))
- item_final: bfloat16 [65536, 64], P(('row', 'col'))
Inputs may be any that keep to these rules, and one draw needn't show every extreme that they name: `block_row`: slot tile rows within one user group; the live slots of a device name distinct tiles. `block_col`: slot tile columns within one item shard. `block_count`: slots at or beyond the count are ignored; some device has all 8 slots live. `block_values`: nonnegative weights; most entries of a tile are zero.
All inputs are finite; a program needn't handle non-finite values.
Results may differ from a plain program's by a relative error of at most 0.0045.
Values may be sent and summed in bfloat16 or wider, within the bound.
No kernel may reach another device: no remote copies, remote signals or barrier semaphores. Data moves between devices by JAX's collectives and lax.ppermute only.
A program may use at most 32 MiB of HBM per device.

v0:
```python
import jax
import jax.numpy as jnp
from jax import lax
from jax.sharding import PartitionSpec as P

LAYERS = 2


def per_device(
    user_emb, item_emb, user_degree, item_degree, block_values, block_row, block_col, block_count
):
    slot_total = block_values.shape[2]
    tile_size = block_values.shape[3]
    width = user_emb.shape[1]
    tile_values = block_values.reshape(slot_total, tile_size, tile_size)
    slot_rows = block_row.reshape(slot_total)
    slot_cols = block_col.reshape(slot_total)
    group_size = user_emb.shape[0] * lax.axis_size("col")
    shard_size = item_emb.shape[0] * lax.axis_size("row")
    num_rows = group_size // tile_size
    num_cols = shard_size // tile_size
    live_slots = jnp.arange(slot_total, dtype=jnp.int32) < block_count.reshape(())
    row_mask = (slot_rows[:, None] == jnp.arange(num_rows, dtype=jnp.int32)[None, :]) & live_slots[
        :, None
    ]
    col_mask = (slot_cols[:, None] == jnp.arange(num_cols, dtype=jnp.int32)[None, :]) & live_slots[
        :, None
    ]
    row_pick = row_mask.astype(jnp.bfloat16)
    col_pick = col_mask.astype(jnp.bfloat16)
    row_weight = row_mask.astype(jnp.float32)
    col_weight = col_mask.astype(jnp.float32)
    highest = lax.Precision.HIGHEST
    user_scale = lax.rsqrt(user_degree.astype(jnp.float32))[:, None]
    item_scale = lax.rsqrt(item_degree.astype(jnp.float32))[:, None]
    users_now = user_emb.astype(jnp.float32)
    items_now = item_emb.astype(jnp.float32)
    user_total = users_now
    item_total = items_now
    sent_group = None
    for layer_index in range(LAYERS):
        sent_items = (item_scale * items_now).astype(jnp.bfloat16)
        item_here = lax.all_gather(sent_items, "row", axis=0, tiled=True)
        sent_users = (user_scale * users_now).astype(jnp.bfloat16)
        sent_group = lax.all_gather(sent_users, "col", axis=0, tiled=True)
        item_pick = jnp.einsum(
            "bc,cte->bte",
            col_pick,
            item_here.reshape(num_cols, tile_size, width),
            preferred_element_type=jnp.float32,
        ).astype(jnp.bfloat16)
        user_pick = jnp.einsum(
            "bu,use->bse",
            row_pick,
            sent_group.reshape(num_rows, tile_size, width),
            preferred_element_type=jnp.float32,
        ).astype(jnp.bfloat16)
        user_prod = jnp.einsum(
            "bst,bte->bse", tile_values, item_pick, preferred_element_type=jnp.float32
        )
        item_prod = jnp.einsum(
            "bst,bse->bte", tile_values, user_pick, preferred_element_type=jnp.float32
        )
        user_part = jnp.einsum("bu,bse->use", row_weight, user_prod, precision=highest)
        item_part = jnp.einsum("bc,bte->cte", col_weight, item_prod, precision=highest)
        user_part, item_part = (
            user_part.reshape(group_size, width),
            item_part.reshape(shard_size, width),
        )
        item_sum = lax.psum_scatter(item_part, "row", scatter_dimension=0, tiled=True)
        items_now = item_scale * item_sum
        users_now = user_scale * lax.psum_scatter(user_part, "col", scatter_dimension=0, tiled=True)
        sent_group = None
        user_total = user_total + users_now
        item_total = item_total + items_now
    return (
        (user_total / (LAYERS + 1.0)).astype(jnp.bfloat16),
        (item_total / (LAYERS + 1.0)).astype(jnp.bfloat16),
    )


def solution(mesh):
    in_specs = (
        P(("row", "col"), None),
        P(("row", "col"), None),
        P(("row", "col")),
        P(("row", "col")),
        P("row", "col", None, None, None),
        P("row", "col", None),
        P("row", "col", None),
        P("row", "col"),
    )
    out_specs = (P(("row", "col"), None), P(("row", "col"), None))
    return jax.shard_map(
        per_device, mesh=mesh, in_specs=in_specs, out_specs=out_specs, check_vma=False
    )
```

profile of v0, /device:TPU:256, one launch (start us, length us, event | category | flops | bytes accessed | tf_op | source)
XLA Modules:
  0.0 2334.9 jit_solution(10700186644285442464)
XLA Ops:
  7.9 0.7 convert_rsqrt_fusion
  8.6 0.8 fusion.24
  9.4 25.4 %all_gather.12 = bf16[512,64]{1,0:T(8,128)(2,1)S(1)} all-gather(bf16[64,64]{1,0:T(8,128)(2,1)S(1)} %fusion.24), channel_id=1, replica_groups=mesh['row'=8,'col'=128] {'row'}, dimensions={0}, use_global_device_ids=true | all-gather | bytes 73728 | tf_op jit(solution)/shard_map/all_gather | solution.py:43
  34.9 0.7 fusion.35
  35.6 0.2 fusion.42
  36.1 0.3 fusion.14
  36.4 1.3 fusion.6
  37.7 2.1 copy.26
  39.9 743.2 %reduce-scatter.5.cloned.1.call-done = f32[32,64]{1,0:T(8,128)} async-done(((f32[4096,64]{1,0:T(8,128)}), f32[32,64]{1,0:T(8,128)}) %reduce-scatter.5.cloned.1.call-update) | async-done | bytes 8208 | tf_op jit(solution)/shard_map/reduce_scatter | solution.py:72
  783.1 0.8 multiply_convert_fusion.1
  783.9 363.0 %all_gather.15 = bf16[4096,64]{1,0:T(8,128)(2,1)S(1)} all-gather(bf16[32,64]{1,0:T(8,128)(2,1)S(1)} %get-tuple-element.4), channel_id=1, replica_groups=mesh['row'=8,'col'=128] {'col'}, dimensions={0}, use_global_device_ids=true | all-gather | bytes 528384 | tf_op jit(solution)/shard_map/all_gather | solution.py:45
  1146.8 0.8 copy.23
  1147.7 0.2 fusion.36
  1147.9 0.2 copy.24
  1148.2 0.2 fusion.8
  1148.4 0.4 fusion
  1148.8 0.8 copy.29
  1149.7 363.3 %all_gather.13 = bf16[4096,64]{1,0:T(8,128)(2,1)S(1)} all-gather(bf16[32,64]{1,0:T(8,128)(2,1)S(1)} %get-tuple-element.5), channel_id=1, replica_groups=mesh['row'=8,'col'=128] {'col'}, dimensions={0}, use_global_device_ids=true | all-gather | bytes 528384 | tf_op jit(solution)/shard_map/all_gather | solution.py:45
  1513.0 0.8 copy.17
  1513.9 0.2 fusion.39
  1514.3 0.2 fusion.12
  1514.6 0.4 fusion.4
  1515.0 0.9 copy.27
  1516.0 41.8 %reduce-scatter.7.cloned.1.call-done = f32[64,64]{1,0:T(8,128)} async-done(((f32[512,64]{1,0:T(8,128)}), f32[64,64]{1,0:T(8,128)}) %reduce-scatter.7.cloned.1.call-update) | async-done | bytes 16400 | tf_op jit(solution)/shard_map/reduce_scatter | solution.py:70
  1557.8 1.5 fusion.27
  1559.2 23.5 %all_gather.14 = bf16[512,64]{1,0:T(8,128)(2,1)S(1)} all-gather(bf16[64,64]{1,0:T(8,128)(2,1)S(1)} %get-tuple-element.3), channel_id=1, replica_groups=mesh['row'=8,'col'=128] {'row'}, dimensions={0}, use_global_device_ids=true | all-gather | bytes 73728 | tf_op jit(solution)/shard_map/all_gather | solution.py:43
  1582.8 0.2 fusion.43
  1583.3 0.3 fusion.10
  1583.6 0.7 fusion.2
  1584.3 2.0 copy.28
  1586.4 740.6 %reduce-scatter.9.cloned.1.call-done = f32[32,64]{1,0:T(8,128)} async-done(((f32[4096,64]{1,0:T(8,128)}), f32[32,64]{1,0:T(8,128)}) %reduce-scatter.9.cloned.1.call-update) | async-done | bytes 8208 | tf_op jit(solution)/shard_map/reduce_scatter | solution.py:72
  2326.9 1.4 fusion.30
  (28 shorter events, 1.1 us)
Async XLA Ops:
  7.2 28.9 %copy-start = (bf16[1,1,8,128,128]{4,3,2,1,0:T(8,128)(2,1)S(1)}, bf16[1,1,8,128,128]{4,3,2,1,0:T(8,128)(2,1)}, u32[]{:S(2)}) copy-start(bf16[1,1,8,128,128]{4,3,2,1,0:T(8,128)(2,1)} %param.12) | copy-start | bytes 786436
  7.2 775.9 %reduce-scatter.5.cloned.1.call-start = ((), (), s32[]{:S(2)}) async-start(), calls=%async_computation.4 | async-start | bytes 2113536 | tf_op jit(solution)/shard_map/reduce_scatter | solution.py:72
  37.7 2.2 copy-start.5
  37.7 745.4 %copy-start.3 = (bf16[32,64]{1,0:T(8,128)(2,1)S(1)}, bf16[32,64]{1,0:T(8,128)(2,1)}, u32[]{:S(2)}) copy-start(bf16[32,64]{1,0:T(8,128)(2,1)} %param.8) | copy-start | bytes 12292
  39.8 1107.9 %copy-start.4 = (s32[1,1,8]{2,1,0:T(1,128)S(1)}, s32[1,1,8]{2,1,0:T(1,128)}, u32[]{:S(2)}) copy-start(s32[1,1,8]{2,1,0:T(1,128)} %param.13) | copy-start | bytes 100
  39.8 1476.1 %reduce-scatter.11.cloned.1.call-start = ((), (), s32[]{:S(2)}) async-start(), calls=%async_computation.7 | async-start | bytes 294912 | tf_op jit(solution)/shard_map/reduce_scatter | solution.py:70
  1149.7 408.1 %reduce-scatter.7.cloned.1.call-start = ((), (), s32[]{:S(2)}) async-start(), calls=%async_computation.5 | async-start | bytes 294912 | tf_op jit(solution)/shard_map/reduce_scatter | solution.py:70
  1513.0 44.8 %copy-start.1 = (bf16[64,64]{1,0:T(8,128)(2,1)S(1)}, bf16[64,64]{1,0:T(8,128)(2,1)}, u32[]{:S(2)}) copy-start(bf16[64,64]{1,0:T(8,128)(2,1)} %param.9) | copy-start | bytes 24580
  1515.9 811.1 %reduce-scatter.9.cloned.1.call-start = ((), (), s32[]{:S(2)}) async-start(), calls=%async_computation.6 | async-start | bytes 2113536 | tf_op jit(solution)/shard_map/reduce_scatter | solution.py:72
  1584.3 742.7 %copy-start.2 = (f32[32,64]{1,0:T(8,128)S(1)}, f32[32,64]{1,0:T(8,128)}, u32[]{:S(2)}) copy-start(f32[32,64]{1,0:T(8,128)} %reduce-scatter.5.cloned.1.call-done) | copy-start | bytes 24580
Sparse Core Ops, SparseCore 0:
  39.9 743.1 reduce-scatter.4
  1149.8 41.4 reduce-scatter.10
  1516.0 41.7 reduce-scatter.6
  1586.5 740.4 reduce-scatter.8
where the time goes:
time: 2340 us; the launch traced here: 2330 us
  waiting for transfers between devices  1530 us (65%)
  blocking collectives  775 us (33%)
    reduce_scatter x2, waiting for transfers between devices, per_device(): lax.psum_scatter(user_part, 'col', scatter_dimension=0, tiled=True)  1480 us
    all_gather x2, blocking collectives, per_device(): sent_group = lax.all_gather(sent_users, 'col', axis=0, tiled=True)  726 us
    all_gather x2, blocking collectives, per_device(): item_here = lax.all_gather(sent_items, 'row', axis=0, tiled=True)  48.9 us
  transfers between devices with their start and end apart: 4, of which 3 were waited for; matrix products, arithmetic and copies ran while one was open for 0% of the time, Pallas kernels for 0%

commit v1 on v0

v1 whole, which is shorter than its diff:
```python
import jax
import jax.numpy as jnp
from jax import lax
from jax.experimental import pallas as pl
from jax.experimental.pallas import tpu as pltpu
from jax.sharding import PartitionSpec as P

EMB = 64
BS = 128
NBLK = 8
F32 = jnp.float32
BF16 = jnp.bfloat16

VMEM = pl.BlockSpec(memory_space=pltpu.VMEM)
SMEM = pl.BlockSpec(memory_space=pltpu.SMEM)
PARAMS = pltpu.CompilerParams(vmem_limit_bytes=24 * 1024 * 1024)


def pack_users(prod):
    parts = []
    for block in range(4):
        base = block * 32
        parts.append(
            jnp.concatenate([prod[base : base + 16, :], prod[base + 16 : base + 32, :]], axis=1)
        )
    return jnp.concatenate(parts, axis=0)


def user_products(rows, cols, count, tiles, items, lane, acc, out):
    out[...] = jnp.zeros_like(out)
    for slot in range(NBLK):
        acc[rows[0, 0, slot]] = jnp.zeros((EMB, BS), F32)
    live_slots = count[0, 0]
    for slot in range(NBLK):
        start = pl.multiple_of(cols[0, 0, slot] * BS, BS)
        prod = jnp.dot(
            tiles[0, 0, slot], items[pl.ds(start, BS), :], preferred_element_type=F32
        )
        packed = pack_users(prod[:, lane : lane + EMB])
        packed = jnp.where(slot < live_slots, packed, 0.0)
        acc[rows[0, 0, slot]] += packed
    for slot in range(NBLK):
        out[rows[0, 0, slot]] = acc[rows[0, 0, slot]].astype(BF16)


def first_users_kernel(rows, cols, count, tiles, items, out, acc):
    user_products(rows, cols, count, tiles, items, 0, acc, out)


def items_kernel(rows, cols, count, tiles, users, out, acc):
    acc[...] = jnp.zeros_like(acc)
    live_slots = count[0, 0]
    for slot in range(NBLK):
        start = pl.multiple_of(rows[0, 0, slot] * BS, BS)
        prod = lax.dot_general(
            tiles[0, 0, slot],
            users[pl.ds(start, BS), :],
            (((0,), (0,)), ((), ())),
            preferred_element_type=F32,
        )
        acc[cols[0, 0, slot]] += jnp.where(slot < live_slots, prod, 0.0)
    out[...] = acc[...].astype(BF16)


def second_users_kernel(
    mine, rows, cols, count, tiles, parts, first, item_emb, out, item_final, acc, sums, sent
):
    total = parts[0].astype(F32)
    for part in range(1, parts.shape[0]):
        total = total + parts[part].astype(F32)
    sums[...] = total
    lanes = lax.broadcasted_iota(jnp.int32, total.shape, 1)
    scale = lax.rsqrt(jnp.where(lanes >= EMB, first[...].astype(F32), 1.0))
    sent[...] = (scale * (scale * total)).astype(BF16)
    own = pl.ds(pl.multiple_of(mine[0] * EMB, EMB), EMB)
    own_scale = lax.rsqrt(first[own, :][:, EMB:].astype(F32))
    own_total = sums[own, :]
    layers = item_emb[...].astype(F32) + own_scale * own_total[:, EMB:]
    layers = layers + own_scale * own_total[:, :EMB]
    item_final[...] = (layers / 3.0).astype(BF16)
    user_products(rows, cols, count, tiles, sent, EMB, acc, out)


def unpack_sum(parts):
    total = jnp.sum(parts[...].astype(F32), axis=0)
    return jnp.concatenate([total[:, :EMB], total[:, EMB:]], axis=0)


def users_between_kernel(parts, scale, sent_first, message, users_one):
    users_now = scale[...] * unpack_sum(parts)
    users_one[...] = users_now
    sent = (scale[...] * users_now).astype(BF16)
    block = jnp.concatenate([sent, sent_first[...]], axis=1)
    message[...] = jnp.broadcast_to(block[None], message.shape)


def users_last_kernel(parts, scale, user_emb, users_one, user_final):
    layers = user_emb[...].astype(F32) + users_one[...]
    layers = layers + scale[...] * unpack_sum(parts)
    user_final[...] = (layers / 3.0).astype(BF16)


def per_device(
    user_emb, item_emb, user_degree, item_degree, block_values, block_row, block_col, block_count
):
    n_row = lax.axis_size("row")
    n_col = lax.axis_size("col")
    u_dev = user_emb.shape[0]
    i_dev = item_emb.shape[0]
    group = u_dev * n_col
    shard = i_dev * n_row
    slots = [SMEM, SMEM, SMEM, VMEM]
    slot_args = (block_row, block_col, block_count, block_values)
    user_scale = lax.rsqrt(user_degree.astype(F32))[:, None]
    item_scale = lax.rsqrt(item_degree.astype(F32))[:, None]
    sent_items = (item_scale * item_emb.astype(F32)).astype(BF16)
    sent_users = (user_scale * user_emb.astype(F32)).astype(BF16)
    user_scale = jnp.broadcast_to(user_scale, (u_dev, EMB))
    degrees = jnp.broadcast_to(item_degree.astype(BF16)[:, None], (i_dev, EMB))

    with jax.named_scope("items_0"):
        first = lax.all_gather(
            jnp.concatenate([sent_items, degrees], axis=1), "row", axis=0, tiled=True
        )
    tile_rows = group // BS
    packed_shape = jax.ShapeDtypeStruct((tile_rows, BS // 2, BS), BF16)
    acc_users = pltpu.VMEM((tile_rows, BS // 2, BS), F32)
    parts = pl.pallas_call(
        first_users_kernel,
        out_shape=packed_shape,
        in_specs=slots + [VMEM],
        out_specs=VMEM,
        scratch_shapes=[acc_users],
        compiler_params=PARAMS,
        name="users_1_parts",
    )(*slot_args, first)
    with jax.named_scope("users_1"):
        parts = lax.all_to_all(
            parts.reshape(n_col, u_dev // 2, BS), "col", split_axis=0, concat_axis=0, tiled=True
        )
    message, users_one = pl.pallas_call(
        users_between_kernel,
        out_shape=(
            jax.ShapeDtypeStruct((n_col, u_dev, BS), BF16),
            jax.ShapeDtypeStruct((u_dev, EMB), F32),
        ),
        in_specs=[VMEM] * 3,
        out_specs=(VMEM, VMEM),
        compiler_params=PARAMS,
        name="users_1_sum",
    )(parts, user_scale, sent_users)
    with jax.named_scope("sent_users"):
        users = lax.all_to_all(message, "col", split_axis=0, concat_axis=0, tiled=True)
    item_parts = pl.pallas_call(
        items_kernel,
        out_shape=jax.ShapeDtypeStruct((shard // BS, BS, BS), BF16),
        in_specs=slots + [VMEM],
        out_specs=VMEM,
        scratch_shapes=[pltpu.VMEM((shard // BS, BS, BS), F32)],
        compiler_params=PARAMS,
        name="items_parts",
    )(*slot_args, users.reshape(group, BS))
    with jax.named_scope("items_1_and_2"):
        item_parts = lax.all_gather(item_parts.reshape(shard, BS), "row", axis=0)
    mine = lax.axis_index("row").astype(jnp.int32).reshape(1)
    parts, item_final = pl.pallas_call(
        second_users_kernel,
        out_shape=(packed_shape, jax.ShapeDtypeStruct((i_dev, EMB), BF16)),
        in_specs=[SMEM] + slots + [VMEM] * 3,
        out_specs=(VMEM, VMEM),
        scratch_shapes=[
            acc_users,
            pltpu.VMEM((shard, BS), F32),
            pltpu.VMEM((shard, BS), BF16),
        ],
        compiler_params=PARAMS,
        name="users_2_parts",
    )(mine, *slot_args, item_parts, first, item_emb)
    with jax.named_scope("users_2"):
        parts = lax.all_to_all(
            parts.reshape(n_col, u_dev // 2, BS), "col", split_axis=0, concat_axis=0, tiled=True
        )
    user_final = pl.pallas_call(
        users_last_kernel,
        out_shape=jax.ShapeDtypeStruct((u_dev, EMB), BF16),
        in_specs=[VMEM] * 4,
        out_specs=VMEM,
        compiler_params=PARAMS,
        name="users_final",
    )(parts, user_scale, user_emb, users_one)
    return user_final, item_final


def solution(mesh):
    in_specs = (
        P(("row", "col"), None),
        P(("row", "col"), None),
        P(("row", "col")),
        P(("row", "col")),
        P("row", "col", None, None, None),
        P("row", "col", None),
        P("row", "col", None),
        P("row", "col"),
    )
    out_specs = (P(("row", "col"), None), P(("row", "col"), None))
    return jax.shard_map(
        per_device, mesh=mesh, in_specs=in_specs, out_specs=out_specs, check_vma=False
    )
```

time: 2340 us -> 201 us (0.09)
  the two profiles are of different devices: /device:TPU:256 before, /device:TPU:1 now
where the time goes in v1:
time: 201 us
  blocking collectives  101 us (50%)
  waiting for transfers between devices  60.8 us (30%)
  between operations  14.8 us (7%)
  starting transfers between devices  14.1 us (7%)
  Pallas kernels  6.07 us (3%)
  local copies, waits for them, and re-layouts  2.35 us (1%)
    all_gather x1, waiting for transfers between devices, per_device(): item_parts = lax.all_gather(item_parts.reshape(shard, BS), 'row', axis=0)  42.1 us
    all_to_all x1, blocking collectives, per_device(): lax.all_to_all(message, 'col', split_axis=0, concat_axis=0, tiled=True)  36.6 us
    all_gather x1, blocking collectives, per_device(): lax.all_gather(jnp.concatenate([sent_items, degrees], axis=1), 'row', axi...  32.3 us
    all_to_all x1, blocking collectives, per_device(): lax.all_to_all(parts.reshape(n_col, u_dev // 2, BS), 'col', split_axis=0,...  32.2 us
    all_to_all x1, waiting for transfers between devices, per_device(): lax.all_to_all(parts.reshape(n_col, u_dev // 2, BS), 'col', split_axis=0,...  18.7 us
    all_to_all x1, starting transfers between devices, per_device(): lax.all_to_all(parts.reshape(n_col, u_dev // 2, BS), 'col', split_axis=0,...  14.1 us
  transfers between devices with their start and end apart: 2, of which 2 were waited for; matrix products, arithmetic and copies ran while one was open for 0% of the time, Pallas kernels for 0%

profile of v1, /device:TPU:1, one launch (start us, length us, event | category | flops | bytes accessed | tf_op | source)
XLA Modules:
  0.0 200.9 jit_solution(10549164935700269987)
XLA Ops:
  7.2 0.0 copy-start.7
  7.2 0.7 convert_element_type.24
  7.9 0.0 copy-done.7
  8.6 0.8 multiply_convert_fusion
  9.4 0.1 broadcast_in_dim.4
  9.4 0.1 pad_maximum_fusion
  9.5 0.0 copy-start.5
  9.5 0.0 copy-start.6
  9.5 32.3 %all_gather.6.items.first = bf16[512,128]{1,0:T(8,128)(2,1)S(1)} all-gather(bf16[64,128]{1,0:T(8,128)(2,1)S(1)} %pad_maximum_fusion), channel_id=1, replica_groups=mesh['row'=8,'col'=128] {'row'}, dimensions={0}, use_global_device_ids=true | all-gather | bytes 147456 | tf_op jit(solution)/shard_map/items_0/all_gather | solution.py:122
  41.8 0.0 copy-done.5
  41.8 0.0 copy-done.6
  41.8 0.9 copy-done
  42.7 1.7 users_1_parts.1
  44.5 14.1 %all-to-all-start = ((bf16[128,16,128]{2,1,0:T(8,128)(2,1)}), bf16[128,16,128]{2,1,0:T(8,128)(2,1)S(1)}, u32[]{:S(2)}, u32[]{:S(2)}) async-start(bf16[128,16,128]{2,1,0:T(8,128)(2,1)} %bitcast.1), calls=%async_computation | async-start | bytes 1048576 | tf_op jit(solution)/shard_map/users_1/all_to_all | solution.py:138
  58.5 0.0 all-gather.2.cloned.1.call-start
  58.6 0.0 copy-done.8
  58.6 0.0 copy-done.4
  58.6 0.1 multiply_convert_fusion.1.sent_first
  58.7 18.7 %all-to-all-done.parts = bf16[128,16,128]{2,1,0:T(8,128)(2,1)S(1)} async-done(((bf16[128,16,128]{2,1,0:T(8,128)(2,1)}), bf16[128,16,128]{2,1,0:T(8,128)(2,1)S(1)}, u32[]{:S(2)}, u32[]{:S(2)}) %all-to-all-start) | async-done | bytes 524320 | tf_op jit(solution)/shard_map/users_1/all_to_all | solution.py:138
  77.4 0.1 broadcast_in_dim.5.scale
  77.5 0.3 users_1_sum.1
  77.8 0.0 copy-start.1
  77.8 36.6 %all_to_all.15 = bf16[128,32,128]{2,1,0:T(8,128)(2,1)S(1)} all-to-all(bf16[128,32,128]{2,1,0:T(8,128)(2,1)S(1)} %get-tuple-element.6), channel_id=1, replica_groups=mesh['row'=8,'col'=128] {'col'}, dimensions={0} | all-to-all | bytes 2097152 | tf_op jit(solution)/shard_map/sent_users/all_to_all | solution.py:153
  114.4 0.0 copy-done.1
  114.4 1.5 items_parts.1
  115.9 0.0 all-gather.2.cloned.1.call-update
  115.9 42.1 %all-gather.2.cloned.1.call-done.parts = bf16[8,512,128]{2,1,0:T(8,128)(2,1)} async-done(((bf16[1,512,128]{2,1,0:T(8,128)(2,1)}), bf16[8,512,128]{2,1,0:T(8,128)(2,1)}) %all-gather.2.cloned.1.call-update) | async-done | bytes 1048592 | tf_op jit(solution)/shard_map/items_1_and_2/all_gather | solution.py:164
  158.0 0.0 copy-done.3
  158.0 1.2 copy-done.2
  159.2 1.8 users_2_parts.1
  161.0 32.2 %all_to_all.16.parts = bf16[128,16,128]{2,1,0:T(8,128)(2,1)S(1)} all-to-all(bf16[128,16,128]{2,1,0:T(8,128)(2,1)S(1)} %bitcast.6), channel_id=1, replica_groups=mesh['row'=8,'col'=128] {'col'}, dimensions={0} | all-to-all | bytes 1048576 | tf_op jit(solution)/shard_map/users_2/all_to_all | solution.py:180
  193.2 0.8 users_final.1
  (7 shorter events, 0.0 us)
Async XLA Ops:
  7.2 0.7 copy-start.7
  9.5 32.3 %copy-start.5 = (s32[1,1,8]{2,1,0:T(1,128)S(1)}, s32[1,1,8]{2,1,0:T(1,128)}, u32[]{:S(2)}) copy-start(s32[1,1,8]{2,1,0:T(1,128)} %rows.5) | copy-start | bytes 100
  9.5 32.3 %copy-start.6 = (s32[1,1,8]{2,1,0:T(1,128)S(1)}, s32[1,1,8]{2,1,0:T(1,128)}, u32[]{:S(2)}) copy-start(s32[1,1,8]{2,1,0:T(1,128)} %cols.5) | copy-start | bytes 100
  41.8 1.0 copy-start
  44.5 14.1 %copy-start.8 = (s32[32]{0:T(128)S(1)}, s32[32]{0:T(128)}, u32[]{:S(2)}) copy-start(s32[32]{0:T(128)} %param.10) | copy-start | bytes 388
  44.5 14.2 %copy-start.4 = (bf16[32,64]{1,0:T(8,128)(2,1)S(1)}, bf16[32,64]{1,0:T(8,128)(2,1)}, u32[]{:S(2)}) copy-start(bf16[32,64]{1,0:T(8,128)(2,1)} %user_emb.1) | copy-start | bytes 12292
  44.5 33.0 %all-to-all-start = ((bf16[128,16,128]{2,1,0:T(8,128)(2,1)}), bf16[128,16,128]{2,1,0:T(8,128)(2,1)S(1)}, u32[]{:S(2)}, u32[]{:S(2)}) async-start(bf16[128,16,128]{2,1,0:T(8,128)(2,1)} %bitcast.1), calls=%async_computation | async-start | bytes 1048576 | tf_op jit(solution)/shard_map/users_1/all_to_all | solution.py:138
  58.5 99.4 %all-gather.2.cloned.1.call-start = ((), (), s32[]{:S(2)}) async-start(), calls=%async_computation.3 | async-start | bytes 1179648 | tf_op jit(solution)/shard_map/items_1_and_2/all_gather | solution.py:164
  77.8 36.6 %copy-start.1 = (bf16[1,1,8,128,128]{4,3,2,1,0:T(8,128)(2,1)S(1)}, bf16[1,1,8,128,128]{4,3,2,1,0:T(8,128)(2,1)}, u32[]{:S(2)}) copy-start(bf16[1,1,8,128,128]{4,3,2,1,0:T(8,128)(2,1)} %tiles.5) | copy-start | bytes 786436
  115.9 42.1 %copy-start.3 = (bf16[64,64]{1,0:T(8,128)(2,1)S(1)}, bf16[64,64]{1,0:T(8,128)(2,1)}, u32[]{:S(2)}) copy-start(bf16[64,64]{1,0:T(8,128)(2,1)} %item_emb.1) | copy-start | bytes 24580
  158.0 1.2 copy-start.2
Sparse Core Ops, SparseCore 0:
  116.0 41.9 all-gather.1

commit v2 on v1

v2 whole, which is shorter than its diff:
```python
import jax
import jax.numpy as jnp
from jax import lax
from jax.experimental import pallas as pl
from jax.experimental.pallas import tpu as pltpu
from jax.sharding import PartitionSpec as P

EMB = 64
BS = 128
NBLK = 8
U_BLOCKS = 4
F32 = jnp.float32
BF16 = jnp.bfloat16

VMEM = pl.BlockSpec(memory_space=pltpu.VMEM)
SMEM = pl.BlockSpec(memory_space=pltpu.SMEM)
PARAMS = pltpu.CompilerParams(vmem_limit_bytes=24 * 1024 * 1024)


def fold(rows):
    half = rows.shape[0] // 2
    return jnp.concatenate([rows[:half, :], rows[half:, :]], axis=1)


def unfold(rows):
    return jnp.concatenate([rows[:, :EMB], rows[:, EMB:]], axis=0)


def user_products(rows, cols, count, tiles, items_of, acc, store):
    for slot in range(NBLK):
        acc[rows[0, 0, slot]] = jnp.zeros(acc.shape[1:], F32)
    for slot in range(NBLK):
        prod = jnp.dot(
            tiles[0, 0, slot], items_of(cols[0, 0, slot]), preferred_element_type=F32
        )
        step = BS // U_BLOCKS
        for block in range(U_BLOCKS):
            folded = fold(prod[block * step : (block + 1) * step, :])
            folded = jnp.where(slot < count[0, 0], folded, 0.0)
            acc[rows[0, 0, slot], block] += folded
    for slot in range(NBLK):
        store(rows[0, 0, slot], acc[rows[0, 0, slot]].astype(BF16))


def item_products(rows, cols, count, tiles, users_of, acc):
    acc[...] = jnp.zeros_like(acc)
    for slot in range(NBLK):
        blocks = users_of(rows[0, 0, slot])
        users = jnp.concatenate([unfold(blocks[block]) for block in range(U_BLOCKS)], axis=0)
        prod = lax.dot_general(
            tiles[0, 0, slot], users, (((0,), (0,)), ((), ())), preferred_element_type=F32
        )
        acc[cols[0, 0, slot]] += jnp.where(slot < count[0, 0], prod, 0.0)


def block_range(tile_row):
    return pl.ds(pl.multiple_of(tile_row * U_BLOCKS, U_BLOCKS), U_BLOCKS)


def tile_range(tile_col):
    return pl.ds(pl.multiple_of(tile_col * BS, BS), BS)


def users_one_kernel(rows, cols, count, tiles, first, out, acc):
    out[...] = jnp.zeros_like(out)

    def store(tile_row, value):
        out[block_range(tile_row)] = value

    user_products(
        rows, cols, count, tiles, lambda col: first[tile_range(col), :][:, EMB:], acc, store
    )


def items_one_kernel(rows, cols, count, tiles, users, out, acc):
    item_products(rows, cols, count, tiles, lambda row: users[block_range(row)], acc)
    for col in range(acc.shape[0]):
        out[col] = fold(acc[col]).astype(BF16)


def middle_kernel(
    mine, rows, cols, count, tiles, item_parts, first, user_parts, user_scale,
    message, users_one, items_one, acc, sent, scaled,
):
    total = item_parts[0].astype(F32)
    for part in range(1, item_parts.shape[0]):
        total = total + item_parts[part].astype(F32)
    for col in range(total.shape[0]):
        here = slice(col * BS, (col + 1) * BS)
        scale = lax.rsqrt(first[here, :][:, :EMB].astype(F32))
        items_now = scale * unfold(total[col])
        scaled[here, :] = items_now
        sent[here, :] = (scale * items_now).astype(BF16)
    own = items_one.shape[0]
    items_one[...] = scaled[pl.ds(pl.multiple_of(mine[0] * own, own), own), :]

    users_now = user_scale[...] * unfold(jnp.sum(user_parts[...].astype(F32), axis=0))
    users_one[...] = users_now
    block = fold((user_scale[...] * users_now).astype(BF16))
    half = block.shape[0]
    message[:, :half, :] = jnp.broadcast_to(block[None], (message.shape[0], half, BS))
    message[:, half:, :] = jnp.zeros((message.shape[0], half, BS), BF16)

    def store(tile_row, value):
        message[block_range(tile_row), half:, :] = value

    user_products(
        rows, cols, count, tiles, lambda col: sent[tile_range(col), :], acc, store
    )


def last_kernel(
    rows, cols, count, tiles, arrived, user_scale, user_emb, users_one, out, user_final, acc
):
    half = arrived.shape[1] // 2
    layers = user_emb[...].astype(F32) + users_one[...]
    parts = arrived[:, half:, :].astype(F32)
    layers = layers + user_scale[...] * unfold(jnp.sum(parts, axis=0))
    user_final[...] = (layers / 3.0).astype(BF16)
    item_products(
        rows, cols, count, tiles, lambda row: arrived[block_range(row), :half, :], acc
    )
    own = 2 * out.shape[1]
    for part in range(out.shape[0]):
        start = part * own
        out[part] = fold(acc[start // BS, start % BS : start % BS + own, :]).astype(BF16)


def items_final_kernel(parts, first, item_emb, items_one, item_final):
    total = parts[0].astype(F32)
    for part in range(1, parts.shape[0]):
        total = total + parts[part].astype(F32)
    scale = lax.rsqrt(first[:, :EMB].astype(F32))
    layers = item_emb[...].astype(F32) + items_one[...] + scale * unfold(total)
    item_final[...] = (layers / 3.0).astype(BF16)


def per_device(
    user_emb, item_emb, user_degree, item_degree, block_values, block_row, block_col, block_count
):
    n_row = lax.axis_size("row")
    n_col = lax.axis_size("col")
    u_dev = user_emb.shape[0]
    i_dev = item_emb.shape[0]
    group = u_dev * n_col
    shard = i_dev * n_row
    tile_rows, tile_cols = group // BS, shard // BS
    slots = [SMEM, SMEM, SMEM, VMEM]
    slot_args = (block_row, block_col, block_count, block_values)
    acc_users = pltpu.VMEM((tile_rows, U_BLOCKS, u_dev // 2, BS), F32)
    acc_items = pltpu.VMEM((tile_cols, BS, EMB), F32)

    user_scale = lax.rsqrt(user_degree.astype(F32))[:, None]
    item_scale = lax.rsqrt(item_degree.astype(F32))[:, None]
    sent_items = (item_scale * item_emb.astype(F32)).astype(BF16)
    sent_users = (user_scale * user_emb.astype(F32)).astype(BF16)
    user_scale = jnp.broadcast_to(user_scale, (u_dev, EMB))
    degrees = jnp.broadcast_to(item_degree.astype(BF16)[:, None], (i_dev, EMB))
    own_first = jnp.concatenate([degrees, sent_items], axis=1)

    with jax.named_scope("users_0"):
        block = jnp.concatenate([sent_users[: u_dev // 2], sent_users[u_dev // 2 :]], axis=1)
        users = lax.all_to_all(
            jnp.broadcast_to(block[None], (n_col, *block.shape)),
            "col", split_axis=0, concat_axis=0, tiled=True,
        )
    with jax.named_scope("items_0"):
        first = lax.all_gather(own_first, "row", axis=0, tiled=True)
    user_parts = pl.pallas_call(
        users_one_kernel,
        out_shape=jax.ShapeDtypeStruct((n_col, u_dev // 2, BS), BF16),
        in_specs=slots + [VMEM],
        out_specs=VMEM,
        scratch_shapes=[acc_users],
        compiler_params=PARAMS,
        name="users_1_parts",
    )(*slot_args, first)
    item_parts = pl.pallas_call(
        items_one_kernel,
        out_shape=jax.ShapeDtypeStruct((tile_cols, BS // 2, BS), BF16),
        in_specs=slots + [VMEM],
        out_specs=VMEM,
        scratch_shapes=[acc_items],
        compiler_params=PARAMS,
        name="items_1_parts",
    )(*slot_args, users)
    with jax.named_scope("users_1"):
        user_parts = lax.all_to_all(user_parts, "col", split_axis=0, concat_axis=0, tiled=True)
    with jax.named_scope("items_1"):
        item_parts = lax.all_gather(item_parts.reshape(shard // 2, BS), "row", axis=0)
    item_parts = item_parts.reshape(n_row, tile_cols, BS // 2, BS)
    mine = lax.axis_index("row").astype(jnp.int32).reshape(1)
    message, users_one, items_one = pl.pallas_call(
        middle_kernel,
        out_shape=(
            jax.ShapeDtypeStruct((n_col, u_dev, BS), BF16),
            jax.ShapeDtypeStruct((u_dev, EMB), F32),
            jax.ShapeDtypeStruct((i_dev, EMB), F32),
        ),
        in_specs=[SMEM] + slots + [VMEM] * 4,
        out_specs=(VMEM, VMEM, VMEM),
        scratch_shapes=[
            acc_users,
            pltpu.VMEM((shard, EMB), BF16),
            pltpu.VMEM((shard, EMB), F32),
        ],
        compiler_params=PARAMS,
        name="users_2_parts",
    )(mine, *slot_args, item_parts, first, user_parts, user_scale)
    with jax.named_scope("users_1_and_2"):
        arrived = lax.all_to_all(message, "col", split_axis=0, concat_axis=0, tiled=True)
    item_parts, user_final = pl.pallas_call(
        last_kernel,
        out_shape=(
            jax.ShapeDtypeStruct((n_row, i_dev // 2, BS), BF16),
            jax.ShapeDtypeStruct((u_dev, EMB), BF16),
        ),
        in_specs=slots + [VMEM] * 4,
        out_specs=(VMEM, VMEM),
        scratch_shapes=[acc_items],
        compiler_params=PARAMS,
        name="items_2_parts",
    )(*slot_args, arrived, user_scale, user_emb, users_one)
    with jax.named_scope("items_2"):
        item_parts = lax.all_to_all(item_parts, "row", split_axis=0, concat_axis=0, tiled=True)
    item_final = pl.pallas_call(
        items_final_kernel,
        out_shape=jax.ShapeDtypeStruct((i_dev, EMB), BF16),
        in_specs=[VMEM] * 4,
        out_specs=VMEM,
        compiler_params=PARAMS,
        name="items_final",
    )(item_parts, own_first, item_emb, items_one)
    return user_final, item_final


def solution(mesh):
    in_specs = (
        P(("row", "col"), None),
        P(("row", "col"), None),
        P(("row", "col")),
        P(("row", "col")),
        P("row", "col", None, None, None),
        P("row", "col", None),
        P("row", "col", None),
        P("row", "col"),
    )
    out_specs = (P(("row", "col"), None), P(("row", "col"), None))
    return jax.shard_map(
        per_device, mesh=mesh, in_specs=in_specs, out_specs=out_specs, check_vma=False
    )
```

time: 201 us -> 166 us (0.83)
  waiting for transfers between devices: 60.8 us -> 0.01 us
  blocking collectives: 101 us -> 121 us
  starting transfers between devices: 14.1 us -> 34 us
  between operations: 14.8 us -> 1.39 us
    all_gather x1 -> x0, waiting for transfers between devices: 42.1 us -> none  [per_device(): item_parts = lax.all_gather(item_parts.reshape(shard, BS), 'row', axis=0)]
    all_gather x1 -> x2, blocking collectives: 32.3 us -> 54.2 us  [the longest x1 31.8 us: per_device(): first = lax.all_gather(own_first, 'row', axis=0, tiled=True)]
    all_to_all x1 -> x2, starting transfers between devices: 14.1 us -> 34 us  [the longest x1 17.9 us: per_device(): lax.all_to_all(jnp.broadcast_to(block[None], (n_col, *block.shape)), 'col...]
    all_to_all x1 -> x2, waiting for transfers between devices: 18.7 us -> 0.01 us  [the longest x1 0.01 us: per_device(): lax.all_to_all(user_parts, 'col', split_axis=0, concat_axis=0, tiled=True)]
    all_to_all x1, blocking collectives: 32.2 us -> 20.2 us  [per_device(): lax.all_to_all(item_parts, 'row', split_axis=0, concat_axis=0, tiled=True)]
    all_to_all x1, blocking collectives: 36.6 us -> 46.6 us  [per_device(): lax.all_to_all(message, 'col', split_axis=0, concat_axis=0, tiled=True)]
    unnamed x18 -> x12, local copies, waits for them, and re-layouts: 2.21 us -> 0.03 us
  transfers between devices with their start and end apart: 2 -> 2, of which waited for: 2 -> 0; matrix products, arithmetic and copies ran while one was open for 0% -> 0% of each run, Pallas kernels for 0% -> 2%
where the time goes in v2:
time: 166 us; the launch traced here: 165 us
  blocking collectives  121 us (73%)
  starting transfers between devices  34 us (20%)
  Pallas kernels  6.12 us (4%)
  other arithmetic  1.68 us (1%)
    all_to_all x1, blocking collectives, per_device(): lax.all_to_all(message, 'col', split_axis=0, concat_axis=0, tiled=True)  46.6 us
    all_gather x1, blocking collectives, per_device(): first = lax.all_gather(own_first, 'row', axis=0, tiled=True)  31.8 us
    all_gather x1, blocking collectives, per_device(): lax.all_gather(item_parts.reshape(shard // 2, BS), 'row', axis=0)  22.4 us
    all_to_all x1, blocking collectives, per_device(): lax.all_to_all(item_parts, 'row', split_axis=0, concat_axis=0, tiled=True)  20.2 us
    all_to_all x1, starting transfers between devices, per_device(): lax.all_to_all(jnp.broadcast_to(block[None], (n_col, *block.shape)), 'col...  17.9 us
    all_to_all x1, starting transfers between devices, per_device(): lax.all_to_all(user_parts, 'col', split_axis=0, concat_axis=0, tiled=True)  16.1 us
  transfers between devices with their start and end apart: 2, of which 0 were waited for; matrix products, arithmetic and copies ran while one was open for 0% of the time, Pallas kernels for 2%

profile of v2, /device:TPU:1, one launch (start us, length us, event | category | flops | bytes accessed | tf_op | source)
XLA Modules:
  0.0 165.3 jit_solution(8626149903062255769)
XLA Ops:
  0.6 0.7 convert_rsqrt_fusion.1
  1.3 0.8 multiply_convert_fusion.1
  2.1 0.1 pad_maximum_fusion.1
  2.1 0.9 broadcast_in_dim.4
  3.0 0.0 copy-start.1
  3.0 0.0 copy-start
  3.0 17.9 %all-to-all-start = ((bf16[128,16,128]{2,1,0:T(8,128)(2,1)}), bf16[128,16,128]{2,1,0:T(8,128)(2,1)S(1)}, u32[]{:S(2)}, u32[]{:S(2)}) async-start(bf16[128,16,128]{2,1,0:T(8,128)(2,1)} %broadcast_in_dim.4), calls=%async_computation | async-start | bytes 1048576 | tf_op jit(solution)/shard_map/users_0/all_to_all | solution.py:163
  20.9 0.0 copy-start.5
  21.6 0.0 copy-done.5
  21.6 0.0 copy-done.1
  21.6 0.1 multiply_convert_fusion
  21.7 0.1 broadcast_in_dim.5
  21.8 0.1 pad_maximum_fusion.first
  21.9 0.0 copy-start.4
  21.9 31.8 %all_gather.7.first = bf16[512,128]{1,0:T(8,128)(2,1)S(1)} all-gather(bf16[64,128]{1,0:T(8,128)(2,1)S(1)} %pad_maximum_fusion.first), channel_id=1, replica_groups=mesh['row'=8,'col'=128] {'row'}, dimensions={0}, use_global_device_ids=true | all-gather | bytes 147456 | tf_op jit(solution)/shard_map/items_0/all_gather | solution.py:168
  53.7 0.0 copy-done
  53.7 0.0 copy-done.3
  53.7 0.0 copy-done.4
  53.7 1.8 %users_1_parts.1 = bf16[128,16,128]{2,1,0:T(8,128)(2,1)} custom-call(s32[1,1,8]{2,1,0:T(1,128)S(1)} %copy-done.3, s32[1,1,8]{2,1,0:T(1,128)S(1)} %copy-done.4, s32[1,1]{1,0:T(1,128)S(6)} %copy.10.count, bf16[1,1,8,128,128]{4,3,2,1,0:T(8,128)(2,1)S(1)} %copy-done, bf16[512,128]{1,0:T(8,128)(2,1)S(1)} %all_gather.7.first), custom_call_target="tpu_custom_call" | custom-call | tf_op jit(solution)/shard_map/users_1_parts/pallas_call | solution.py:169
  55.5 0.0 all-to-all-done.users
  55.5 16.1 %all-to-all-start.1 = ((bf16[128,16,128]{2,1,0:T(8,128)(2,1)}), bf16[128,16,128]{2,1,0:T(8,128)(2,1)S(1)}, u32[]{:S(2)}, u32[]{:S(2)}) async-start(bf16[128,16,128]{2,1,0:T(8,128)(2,1)} %users_1_parts.1), calls=%async_computation.1 | async-start | bytes 1048576 | tf_op jit(solution)/shard_map/users_1/all_to_all | solution.py:188
  71.6 1.0 items_1_parts.1
  72.6 22.4 %all_gather.6 = bf16[8,256,128]{2,1,0:T(8,128)(2,1)S(1)} all-gather(bf16[1,256,128]{2,1,0:T(8,128)(2,1)S(1)} %bitcast.4), channel_id=1, replica_groups=mesh['row'=8,'col'=128] {'row'}, dimensions={0}, use_global_device_ids=true | all-gather | bytes 589824 | tf_op jit(solution)/shard_map/items_1/all_gather | solution.py:190
  95.0 0.0 all-to-all-done.1.user_parts
  95.0 0.1 mul.16.user_scale
  95.1 1.2 users_2_parts.1
  96.2 0.0 copy-start.2
  96.2 46.6 %all_to_all.20.arrived = bf16[128,32,128]{2,1,0:T(8,128)(2,1)S(1)} all-to-all(bf16[128,32,128]{2,1,0:T(8,128)(2,1)S(1)} %get-tuple-element.7), channel_id=1, replica_groups=mesh['row'=8,'col'=128] {'col'}, dimensions={0} | all-to-all | bytes 2097152 | tf_op jit(solution)/shard_map/users_1_and_2/all_to_all | solution.py:211
  142.8 0.0 copy-done.2
  142.9 1.5 items_2_parts.1
  144.4 20.2 %all_to_all.21.parts = bf16[8,32,128]{2,1,0:T(8,128)(2,1)S(1)} all-to-all(bf16[8,32,128]{2,1,0:T(8,128)(2,1)S(1)} %get-tuple-element.10), channel_id=1, replica_groups=mesh['row'=8,'col'=128] {'row'}, dimensions={0} | all-to-all | bytes 131072 | tf_op jit(solution)/shard_map/items_2/all_to_all | solution.py:225
  164.6 0.7 items_final.1
  (4 shorter events, 0.0 us)
Async XLA Ops:
  3.0 18.6 %copy-start.1 = (bf16[64,64]{1,0:T(8,128)(2,1)S(1)}, bf16[64,64]{1,0:T(8,128)(2,1)}, u32[]{:S(2)}) copy-start(bf16[64,64]{1,0:T(8,128)(2,1)} %item_emb.1) | copy-start | bytes 24580
  3.0 50.7 %copy-start = (bf16[1,1,8,128,128]{4,3,2,1,0:T(8,128)(2,1)S(1)}, bf16[1,1,8,128,128]{4,3,2,1,0:T(8,128)(2,1)}, u32[]{:S(2)}) copy-start(bf16[1,1,8,128,128]{4,3,2,1,0:T(8,128)(2,1)} %tiles.7) | copy-start | bytes 786436
  3.0 52.5 %all-to-all-start = ((bf16[128,16,128]{2,1,0:T(8,128)(2,1)}), bf16[128,16,128]{2,1,0:T(8,128)(2,1)S(1)}, u32[]{:S(2)}, u32[]{:S(2)}) async-start(bf16[128,16,128]{2,1,0:T(8,128)(2,1)} %broadcast_in_dim.4), calls=%async_computation | async-start | bytes 1048576 | tf_op jit(solution)/shard_map/users_0/all_to_all | solution.py:163
  20.9 0.7 copy-start.5
  21.9 31.8 %copy-start.3 = (s32[1,1,8]{2,1,0:T(1,128)S(1)}, s32[1,1,8]{2,1,0:T(1,128)}, u32[]{:S(2)}) copy-start(s32[1,1,8]{2,1,0:T(1,128)} %rows.7) | copy-start | bytes 100
  21.9 31.8 %copy-start.4 = (s32[1,1,8]{2,1,0:T(1,128)S(1)}, s32[1,1,8]{2,1,0:T(1,128)}, u32[]{:S(2)}) copy-start(s32[1,1,8]{2,1,0:T(1,128)} %cols.7) | copy-start | bytes 100
  55.5 39.5 %all-to-all-start.1 = ((bf16[128,16,128]{2,1,0:T(8,128)(2,1)}), bf16[128,16,128]{2,1,0:T(8,128)(2,1)S(1)}, u32[]{:S(2)}, u32[]{:S(2)}) async-start(bf16[128,16,128]{2,1,0:T(8,128)(2,1)} %users_1_parts.1), calls=%async_computation.1 | async-start | bytes 1048576 | tf_op jit(solution)/shard_map/users_1/all_to_all | solution.py:188
  96.2 46.6 %copy-start.2 = (bf16[32,64]{1,0:T(8,128)(2,1)S(1)}, bf16[32,64]{1,0:T(8,128)(2,1)}, u32[]{:S(2)}) copy-start(bf16[32,64]{1,0:T(8,128)(2,1)} %user_emb.1) | copy-start | bytes 12292

commit v3 on v0

v3 whole, which is shorter than its diff:
```python
import jax
import jax.numpy as jnp
from jax import lax
from jax.experimental import pallas as pl
from jax.experimental.pallas import tpu as pltpu
from jax.sharding import Mesh, PartitionSpec as P

BS = 128
NBLK = 8
F32 = jnp.float32
BF16 = jnp.bfloat16
ROW = ("zh", "co")
PLANE = ("zl", "y")
AXES = ROW + PLANE + ("x",)

VMEM = pl.BlockSpec(memory_space=pltpu.VMEM)
HBM = pl.BlockSpec(memory_space=pltpu.HBM)
SMEM = pl.BlockSpec(memory_space=pltpu.SMEM)


def call(kernel, name, out_shape, in_specs, scratch=(), vmem=24):
    return pl.pallas_call(
        kernel,
        out_shape=out_shape,
        in_specs=in_specs,
        out_specs=jax.tree.map(lambda _: VMEM, out_shape),
        scratch_shapes=scratch,
        compiler_params=pltpu.CompilerParams(vmem_limit_bytes=vmem * 1024 * 1024),
        name=name,
    )


def fetch(pairs, sems):
    copies = [pltpu.make_async_copy(src, dst, sems.at[i]) for i, (src, dst) in enumerate(pairs)]
    for copy in copies:
        copy.start()
    return copies


def start_kernel(
    item_emb, user_emb, item_degree, user_degree, rows, cols, count, tiles, out,
    items, users, item_deg, user_deg, slot_rows, slot_cols, live, sems,
):
    share, size = out.shape[0], tiles.shape[0]
    i_dev, emb = item_emb.shape
    u_dev = user_emb.shape[0]
    step = emb // share
    pairs = [
        (item_emb, items),
        (user_emb, users),
        (item_degree, item_deg),
        (user_degree, user_deg),
        (rows, slot_rows),
        (cols, slot_cols),
        (count, live),
    ]
    small = len(pairs)
    pairs += [(tiles, out.at[to, pl.ds(2 * step, size), :]) for to in range(share)]
    copies = fetch(pairs, sems)
    for copy in copies[:small]:
        copy.wait()
    values = jnp.concatenate(
        [
            items[...].astype(F32),
            users[...].astype(F32),
            jnp.zeros((BS - i_dev - u_dev, emb), F32),
        ],
        axis=0,
    ).T
    extra = jnp.concatenate(
        [
            item_deg[...],
            user_deg[...],
            slot_rows[0],
            slot_cols[0],
            live[...],
            jnp.zeros((1, BS - i_dev - u_dev - 2 * NBLK - 1), jnp.int32),
        ],
        axis=1,
    ).astype(F32)
    for to in range(share):
        out[to, :step, :] = values[to * step : (to + 1) * step, :].astype(BF16)
        out[to, step : 2 * step, :] = jnp.broadcast_to(extra, (step, BS)).astype(BF16)
    for copy in copies[small:]:
        copy.wait()


def users_zero_kernel(i_dev, arrived, message, user_zero, user_scale):
    share, step = arrived.shape[0], message.shape[1]
    u_dev = BS // share
    lanes = slice(i_dev, i_dev + u_dev)
    first = jnp.concatenate([arrived[x, :step, :].astype(F32)[:, lanes] for x in range(share)], 1)
    degree = jnp.concatenate([arrived[x, step : 2 * step, :].astype(F32)[:, lanes] for x in range(share)], 1)
    scale = lax.rsqrt(degree)
    user_zero[...] = first
    user_scale[...] = scale
    message[...] = jnp.broadcast_to((scale * first).astype(BF16)[None], message.shape)


def slot_list(slots, arrived):
    first = arrived.shape[1] - NBLK * BS
    for x in range(arrived.shape[0]):
        for slot in range(NBLK):
            live = slot < slots[x, 2 * NBLK]
            tile = arrived[x, first + slot * BS : first + (slot + 1) * BS, :]
            yield x, slots[x, slot], slots[x, NBLK + slot], live, tile


def item_products(slots, arrived, users, acc):
    acc[...] = jnp.zeros_like(acc)
    for x, row, col, live, tile in slot_list(slots, arrived):
        prod = jnp.dot(users[row], tile, preferred_element_type=F32)
        acc[x, col] += jnp.where(live, prod, 0.0)


def items_one_kernel(slots, arrived, users, out, acc):
    item_products(slots, arrived, users, acc)
    share, tile_cols = acc.shape[:2]
    for x in range(share):
        for col in range(tile_cols):
            out[x * tile_cols + col] = acc[x, col].astype(BF16)
    step = acc.shape[2]
    half = BS // 2
    base = share * tile_cols
    for pair in range(share // 2):
        two = [arrived[2 * pair + k, : 2 * step].astype(F32)[:, :half] for k in range(2)]
        first = jnp.concatenate([both[:step] for both in two], axis=1)
        degree = jnp.concatenate([both[step:] for both in two], axis=1)
        out[base + pair] = (lax.rsqrt(degree) * first).astype(BF16)
        out[base + share // 2 + pair] = degree.astype(BF16)


def users_kernel(slots, arrived, gathered, out, item_sum, acc, sent):
    share, tile_cols, step = item_sum.shape[:3]
    n_row = gathered.shape[0]
    half = BS // 2
    base = share * tile_cols

    def of_tile(block, x, col):
        pair, side = block + x // 2, (x % 2) * half
        return jnp.concatenate(
            [gathered[2 * col + k, pair].astype(F32)[:, side : side + half] for k in range(2)],
            axis=1,
        )

    for x in range(share):
        for col in range(tile_cols):
            at = x * tile_cols + col
            total = gathered[0, at].astype(F32)
            for part in range(1, n_row):
                total = total + gathered[part, at].astype(F32)
            item_sum[x, col] = total
            scale = lax.rsqrt(of_tile(base + share // 2, x, col))
            sent[x, col, :step] = of_tile(base, x, col).astype(BF16)
            sent[x, col, step:] = (scale * (scale * total)).astype(BF16)
    acc[...] = jnp.zeros_like(acc)
    for x, row, col, live, tile in slot_list(slots, arrived):
        prod = lax.dot_general(
            sent[x, col], tile, (((1,), (1,)), ((), ())), preferred_element_type=F32
        )
        acc[row] += jnp.where(live, prod, 0.0)
    out[...] = acc[...].astype(BF16)


def users_sum_kernel(parts, user_zero, user_scale, message, user_final):
    step = message.shape[1]
    total = parts[0].astype(F32)
    for part in range(1, parts.shape[0]):
        total = total + parts[part].astype(F32)
    scale = user_scale[...]
    users_one = scale * total[:step]
    users_two = scale * total[step:]
    message[...] = jnp.broadcast_to((scale * users_one).astype(BF16)[None], message.shape)
    user_final[...] = (user_zero[...] + users_one + users_two) / 3.0


def items_two_kernel(slots, arrived, users, item_sum, user_final, out, acc):
    item_products(slots, arrived, users, acc)
    share, tile_cols, step = acc.shape[:3]
    n_row = 2 * tile_cols
    half = BS // 2
    u_dev = BS // share
    for x in range(share):
        own = user_final[...][:, x * u_dev : (x + 1) * u_dev]
        for col in range(tile_cols):
            total = acc[x, col] + item_sum[x, col] * (1.0 / n_row)
            for k in range(2):
                block = jnp.concatenate(
                    [total[:, k * half : (k + 1) * half], own, jnp.zeros((step, half - u_dev), F32)],
                    axis=1,
                )
                out[2 * col + k, x] = block.astype(BF16)


def final_kernel(
    mine, arrived, item_emb, item_degree, item_final, user_final, items, item_deg, sems
):
    copies = fetch([(item_emb, items), (item_degree, item_deg)], sems)
    n_row, share, step = arrived.shape[:3]
    i_dev, emb = item_emb.shape
    u_dev = user_final.shape[0]
    total = arrived[0].astype(F32)
    for part in range(1, n_row):
        total = total + arrived[part].astype(F32)
    total = total.reshape(emb, BS)
    for copy in copies:
        copy.wait()
    scale = lax.rsqrt(item_deg[...].astype(F32))
    users = arrived[mine[0]].astype(F32).reshape(emb, BS)
    both = jnp.concatenate(
        [total[:, :i_dev] * scale, users[:, i_dev:]], axis=1
    ).T
    item_final[...] = ((items[...].astype(F32) + both[:i_dev]) / 3.0).astype(BF16)
    user_final[...] = both[i_dev : i_dev + u_dev].astype(BF16)


def exchange(values, axes):
    return lax.all_to_all(values, axes, split_axis=0, concat_axis=0, tiled=True)


def per_device(
    user_emb, item_emb, user_degree, item_degree, block_values, block_row, block_col, block_count
):
    share = lax.axis_size("x")
    n_row = lax.axis_size(ROW)
    tile_rows = lax.axis_size(PLANE)
    u_dev, emb = user_emb.shape
    i_dev = item_emb.shape[0]
    tile_cols = i_dev * n_row // BS
    step = emb // share
    shape = jax.ShapeDtypeStruct
    acc_items = pltpu.VMEM((share, tile_cols, step, BS), F32)

    item_degree = item_degree.reshape(1, i_dev)
    message = call(
        start_kernel,
        "start",
        shape((share, 2 * step + NBLK * BS, BS), BF16),
        [HBM] * 8,
        [
            pltpu.VMEM((i_dev, emb), BF16),
            pltpu.VMEM((u_dev, emb), BF16),
            pltpu.VMEM((1, i_dev), jnp.int32),
            pltpu.VMEM((1, u_dev), jnp.int32),
            pltpu.VMEM((1, 1, NBLK), jnp.int32),
            pltpu.VMEM((1, 1, NBLK), jnp.int32),
            pltpu.VMEM((1, 1), jnp.int32),
            pltpu.SemaphoreType.DMA((7 + share,)),
        ],
        vmem=60,
    )(
        item_emb, user_emb, item_degree, user_degree.reshape(1, u_dev),
        block_row, block_col, block_count, block_values.reshape(NBLK * BS, BS),
    )
    with jax.named_scope("base_and_tiles_along_x"):
        arrived = exchange(message, "x")
    first_slot = i_dev + u_dev
    slots = arrived[:, step, first_slot : first_slot + 2 * NBLK + 1].astype(jnp.int32)
    message, user_zero, user_scale = call(
        lambda *refs: users_zero_kernel(i_dev, *refs),
        "users_0",
        (shape((tile_rows, step, BS), BF16), shape((step, BS), F32), shape((step, BS), F32)),
        [VMEM],
    )(arrived)
    with jax.named_scope("sent_users_0"):
        users = exchange(message, PLANE)
    blocks = share * tile_cols + share
    message = call(
        items_one_kernel,
        "items_1_parts",
        shape((blocks, step, BS), BF16),
        [SMEM] + [VMEM] * 2,
        [acc_items],
    )(slots, arrived, users)
    with jax.named_scope("items_0_and_1"):
        gathered = lax.all_gather(message, ROW, axis=0)
    message, item_sum = call(
        users_kernel,
        "users_1_and_2_parts",
        (shape((tile_rows, 2 * step, BS), BF16), shape((share, tile_cols, step, BS), F32)),
        [SMEM] + [VMEM] * 2,
        [
            pltpu.VMEM((tile_rows, 2 * step, BS), F32),
            pltpu.VMEM((share, tile_cols, 2 * step, BS), BF16),
        ],
    )(slots, arrived, gathered)
    with jax.named_scope("users_1_and_2"):
        parts = exchange(message, PLANE)
    message, user_final = call(
        users_sum_kernel,
        "users_sum",
        (shape((tile_rows, step, BS), BF16), shape((step, BS), F32)),
        [VMEM] * 3,
    )(parts, user_zero, user_scale)
    with jax.named_scope("sent_users_1"):
        users = exchange(message, PLANE)
    message = call(
        items_two_kernel,
        "items_2_parts",
        shape((n_row, share, step, BS), BF16),
        [SMEM] + [VMEM] * 4,
        [acc_items],
    )(slots, arrived, users, item_sum, user_final)
    with jax.named_scope("items_2"):
        parts = exchange(message.reshape(n_row * share, step, BS), ROW + ("x",))
    mine = lax.axis_index(ROW).astype(jnp.int32).reshape(1)
    item_final, user_final = call(
        final_kernel,
        "final",
        (shape((i_dev, emb), BF16), shape((u_dev, emb), BF16)),
        [SMEM, VMEM, HBM, HBM],
        [
            pltpu.VMEM((i_dev, emb), BF16),
            pltpu.VMEM((1, i_dev), jnp.int32),
            pltpu.SemaphoreType.DMA((2,)),
        ],
    )(mine, parts.reshape(n_row, share, step, BS), item_emb, item_degree)
    return user_final, item_final


def solution(mesh):
    fine = Mesh(mesh.devices.reshape(4, 2, 4, 8, 4), AXES)
    col = PLANE + ("x",)
    in_specs = (
        P(AXES, None),
        P(AXES, None),
        P(AXES),
        P(AXES),
        P(ROW, col, None, None, None),
        P(ROW, col, None),
        P(ROW, col, None),
        P(ROW, col),
    )
    out_specs = (P(AXES, None), P(AXES, None))
    return jax.shard_map(
        per_device, mesh=fine, in_specs=in_specs, out_specs=out_specs, check_vma=False
    )
```

time: 2340 us -> 141 us (0.06)
  the two profiles are of different devices: /device:TPU:256 before, /device:TPU:1 now
where the time goes in v3:
time: 141 us
  blocking collectives  79.5 us (56%)
  starting transfers between devices  26.2 us (19%)
  waiting for transfers between devices  25.6 us (18%)
  Pallas kernels  8.16 us (6%)
    all_to_all x3, blocking collectives, exchange(): return lax.all_to_all(values, axes, split_axis=0, concat_axis=0, tiled=True)  43.7 us
    all_gather x1, blocking collectives, per_device(): gathered = lax.all_gather(message, ROW, axis=0)  35.7 us
    all_to_all x2, starting transfers between devices, exchange(): return lax.all_to_all(values, axes, split_axis=0, concat_axis=0, tiled=True)  26.2 us
    all_to_all x2, waiting for transfers between devices, exchange(): return lax.all_to_all(values, axes, split_axis=0, concat_axis=0, tiled=True)  25.6 us
  transfers between devices with their start and end apart: 2, of which 2 were waited for; matrix products, arithmetic and copies ran while one was open for 0% of the time, Pallas kernels for 0%

profile of v3, /device:TPU:1, one launch (start us, length us, event | category | flops | bytes accessed | tf_op | source)
XLA Modules:
  0.0 140.8 jit_solution(3734129308057009163)
XLA Ops:
  1.3 2.6 %start.1 = bf16[4,1056,128]{2,1,0:T(8,128)(2,1)} custom-call(bf16[64,64]{1,0:T(8,128)(2,1)} %item_emb.3, bf16[32,64]{1,0:T(8,128)(2,1)} %user_emb.1, s32[1,64]{1,0:T(1,128)} %bitcast.13, s32[1,32]{1,0:T(1,128)} %bitcast.16, s32[1,1,8]{2,1,0:T(1,128)} %rows.1, s32[1,1,8]{2,1,0:T(1,128)} %cols.1, s32[1,1]{1,0:T(1,128)S(6)} %copy.10.count, ...), custom_call_target="tpu_custom_call" | custom-call | tf_op jit(solution)/shard_map/start/pallas_call | solution.py:235
  3.9 14.8 %all_to_all.25.refs_0_.arrived = bf16[4,1056,128]{2,1,0:T(8,128)(2,1)S(1)} all-to-all(bf16[4,1056,128]{2,1,0:T(8,128)(2,1)} %start.1), channel_id=1, replica_groups=mesh['zh'=4,'co'=2,'zl'=4,'y'=8,'x'=4] {'x'}, dimensions={0} | all-to-all | bytes 2162688 | tf_op jit(solution)/shard_map/base_and_tiles_along_x/all_to_all | solution.py:218
  18.7 0.7 users_0.1
  19.4 17.0 %all-to-all-start.1 = ((bf16[32,16,128]{2,1,0:T(8,128)(2,1)}), bf16[32,16,128]{2,1,0:T(8,128)(2,1)S(1)}, u32[]{:S(2)}, u32[]{:S(2)}) async-start(bf16[32,16,128]{2,1,0:T(8,128)(2,1)} %get-tuple-element.11), calls=%async_computation.1 | async-start | bytes 262144 | tf_op jit(solution)/shard_map/sent_users_0/all_to_all | solution.py:218
  36.4 0.1 slice_convert_fusion
  36.5 9.3 %all-to-all-done.1.users = bf16[32,16,128]{2,1,0:T(8,128)(2,1)S(1)} async-done(((bf16[32,16,128]{2,1,0:T(8,128)(2,1)}), bf16[32,16,128]{2,1,0:T(8,128)(2,1)S(1)}, u32[]{:S(2)}, u32[]{:S(2)}) %all-to-all-start.1) | async-done | bytes 131104 | tf_op jit(solution)/shard_map/sent_users_0/all_to_all | solution.py:218
  45.9 1.0 items_1_parts.1
  46.8 35.7 %all-gather = bf16[160,16,128]{2,1,0:T(8,128)(2,1)S(1)} all-gather(bf16[20,16,128]{2,1,0:T(8,128)(2,1)S(1)} %items_1_parts.1), channel_id=2, replica_groups=mesh['zh'=4,'co'=2,'zl'=4,'y'=8,'x'=4] {'zh','co'}, dimensions={0}, use_global_device_ids=true | all-gather | bytes 737280 | tf_op jit(solution)/shard_map/items_0_and_1/all_gather | solution.py:276
  82.6 1.3 users_1_and_2_parts.1
  83.9 14.8 %all_to_all.26.parts = bf16[32,32,128]{2,1,0:T(8,128)(2,1)S(1)} all-to-all(bf16[32,32,128]{2,1,0:T(8,128)(2,1)S(1)} %get-tuple-element.12), channel_id=1, replica_groups=mesh['zh'=4,'co'=2,'zl'=4,'y'=8,'x'=4] {'zl','y'}, dimensions={0} | all-to-all | bytes 524288 | tf_op jit(solution)/shard_map/users_1_and_2/all_to_all | solution.py:218
  98.7 0.1 users_sum.1
  98.8 0.0 copy-start
  98.8 0.0 copy-start.1
  98.8 14.1 %all_to_all.27.users = bf16[32,16,128]{2,1,0:T(8,128)(2,1)S(1)} all-to-all(bf16[32,16,128]{2,1,0:T(8,128)(2,1)S(1)} %get-tuple-element.15), channel_id=1, replica_groups=mesh['zh'=4,'co'=2,'zl'=4,'y'=8,'x'=4] {'zl','y'}, dimensions={0} | all-to-all | bytes 262144 | tf_op jit(solution)/shard_map/sent_users_1/all_to_all | solution.py:218
  113.0 1.7 %items_2_parts.1 = bf16[8,4,16,128]{3,2,1,0:T(8,128)(2,1)} custom-call(s32[4,17]{1,0:T(4,128)S(1)} %bitcast.12, bf16[4,1056,128]{2,1,0:T(8,128)(2,1)S(1)} %all_to_all.25.refs_0_.arrived, bf16[32,16,128]{2,1,0:T(8,128)(2,1)S(1)} %all_to_all.27.users, f32[4,4,16,128]{3,2,1,0:T(8,128)S(1)} %get-tuple-element.16.item_sum, f32[16,128]{1,0:T(8,128)S(1)} %get-tuple-element.17.user_final), custom_call_target="tpu_custom_call" | custom-call | tf_op jit(solution)/shard_map/items_2_parts/pallas_call | solution.py:297
  114.7 9.1 %all-to-all-start.4 = ((bf16[32,16,128]{2,1,0:T(8,128)(2,1)}), bf16[32,16,128]{2,1,0:T(8,128)(2,1)S(1)}, u32[]{:S(2)}, u32[]{:S(2)}) async-start(bf16[32,16,128]{2,1,0:T(8,128)(2,1)} %bitcast.6), calls=%async_computation.4 | async-start | bytes 262144 | tf_op jit(solution)/shard_map/items_2/all_to_all | solution.py:218
  123.8 16.2 %all-to-all-done.4 = bf16[32,16,128]{2,1,0:T(8,128)(2,1)S(1)} async-done(((bf16[32,16,128]{2,1,0:T(8,128)(2,1)}), bf16[32,16,128]{2,1,0:T(8,128)(2,1)S(1)}, u32[]{:S(2)}, u32[]{:S(2)}) %all-to-all-start.4) | async-done | bytes 131104 | tf_op jit(solution)/shard_map/items_2/all_to_all | solution.py:218
  140.0 0.0 copy-done
  140.0 0.0 copy-done.1
  140.0 0.8 final.1
Async XLA Ops:
  19.4 26.5 %all-to-all-start.1 = ((bf16[32,16,128]{2,1,0:T(8,128)(2,1)}), bf16[32,16,128]{2,1,0:T(8,128)(2,1)S(1)}, u32[]{:S(2)}, u32[]{:S(2)}) async-start(bf16[32,16,128]{2,1,0:T(8,128)(2,1)} %get-tuple-element.11), calls=%async_computation.1 | async-start | bytes 262144 | tf_op jit(solution)/shard_map/sent_users_0/all_to_all | solution.py:218
  98.8 41.2 %copy-start = (bf16[64,64]{1,0:T(8,128)(2,1)S(1)}, bf16[64,64]{1,0:T(8,128)(2,1)}, u32[]{:S(2)}) copy-start(bf16[64,64]{1,0:T(8,128)(2,1)} %item_emb.3) | copy-start | bytes 24580
  98.8 41.2 %copy-start.1 = (s32[64]{0:T(128)S(1)}, s32[64]{0:T(128)}, u32[]{:S(2)}) copy-start(s32[64]{0:T(128)} %param.11) | copy-start | bytes 772
  114.7 25.4 %all-to-all-start.4 = ((bf16[32,16,128]{2,1,0:T(8,128)(2,1)}), bf16[32,16,128]{2,1,0:T(8,128)(2,1)S(1)}, u32[]{:S(2)}, u32[]{:S(2)}) async-start(bf16[32,16,128]{2,1,0:T(8,128)(2,1)} %bitcast.6), calls=%async_computation.4 | async-start | bytes 262144 | tf_op jit(solution)/shard_map/items_2/all_to_all | solution.py:218

commit v4 on v3

v4 whole, which is shorter than its diff:
```python
import jax
import jax.numpy as jnp
from jax import lax
from jax.experimental import pallas as pl
from jax.experimental.pallas import tpu as pltpu
from jax.sharding import Mesh, PartitionSpec as P

BS = 128
NBLK = 8
F32 = jnp.float32
BF16 = jnp.bfloat16
ROW = ("zh", "co")
PLANE = ("zl", "y")
AXES = ROW + PLANE + ("x",)

VMEM = pl.BlockSpec(memory_space=pltpu.VMEM)
HBM = pl.BlockSpec(memory_space=pltpu.HBM)
SMEM = pl.BlockSpec(memory_space=pltpu.SMEM)


def call(kernel, name, out_shape, in_specs, scratch=(), out_specs=None, vmem=24):
    return pl.pallas_call(
        kernel,
        out_shape=out_shape,
        in_specs=in_specs,
        out_specs=out_specs or jax.tree.map(lambda _: VMEM, out_shape),
        scratch_shapes=scratch,
        compiler_params=pltpu.CompilerParams(vmem_limit_bytes=vmem * 1024 * 1024),
        name=name,
    )


def fetch(pairs, sems, first):
    copies = [
        pltpu.make_async_copy(src, dst, sems.at[first + i]) for i, (src, dst) in enumerate(pairs)
    ]
    for copy in copies:
        copy.start()
    return copies


def columns_of(values, to, step):
    half = values.shape[0] // 2
    run = step // 2
    low = values[to * run : (to + 1) * run, :]
    return jnp.concatenate([low, values[half + to * run : half + (to + 1) * run, :]], axis=0)


def start_kernel(
    item_emb, user_emb, item_degree, user_degree, rows, cols, count, tiles, payload, message,
    items, users, item_deg, user_deg, slot_rows, slot_cols, live, held, base, sems,
):
    share = message.shape[1]
    i_dev, emb = item_emb.shape
    u_dev = user_emb.shape[0]
    step = emb // share
    small = [
        (item_emb, items),
        (user_emb, users),
        (item_degree, item_deg),
        (user_degree, user_deg),
        (rows, slot_rows),
        (cols, slot_cols),
        (count, live),
    ]
    (fetched,) = fetch([(tiles, held)], sems, len(small))
    ready = fetch(small, sems, 0)
    for copy in ready:
        copy.wait()
    values = jnp.concatenate(
        [
            items[...].astype(F32),
            users[...].astype(F32),
            jnp.zeros((BS - i_dev - u_dev, emb), F32),
        ],
        axis=0,
    ).T
    extra = jnp.concatenate(
        [
            item_deg[...],
            user_deg[...],
            slot_rows[0],
            slot_cols[0],
            live[0],
            jnp.zeros((1, BS - i_dev - u_dev - 2 * NBLK - 1), jnp.int32),
        ],
        axis=1,
    ).astype(F32)
    base[share] = jnp.broadcast_to(extra, (step, BS)).astype(BF16)
    scale = lax.rsqrt(user_deg[...].astype(F32))
    for to in range(share):
        columns = columns_of(values, to, step)
        base[to] = columns.astype(BF16)
        sent = scale * columns[:, i_dev : i_dev + u_dev]
        low, high = sent[: step // 2], sent[step // 2 :]
        block = jnp.concatenate([low, low, high, high], axis=1).astype(BF16)
        message[:, to] = jnp.broadcast_to(block[None], (message.shape[0], *block.shape))
    fetched.wait()
    last = fetch(
        [
            (base, payload.at[pl.ds(0, share + 1)]),
            (held, payload.at[pl.ds(share + 1, held.shape[0])]),
        ],
        sems,
        len(small) + 1,
    )
    for copy in last:
        copy.wait()


def slot_list(place, slots, payloads):
    share = len(payloads)
    for away, payload in enumerate(payloads):
        x = lax.rem(place[1] + (share - away), share)
        step = payload.shape[1]
        blocks = BS // step
        for slot in range(NBLK):
            live = slot < slots[away, 2 * NBLK]
            first = share + 1 + slot * blocks
            tile = payload[first : first + blocks].reshape(BS, BS)
            yield x, slots[away, slot], slots[away, NBLK + slot], live, tile


def item_products(place, slots, payloads, users, acc):
    acc[...] = jnp.zeros_like(acc)
    for x, row, col, live, tile in slot_list(place, slots, payloads):
        prod = jnp.dot(users[row], tile, preferred_element_type=F32)
        acc[x, col] += jnp.where(live, prod, 0.0)


def items_one_kernel(
    place, slots, p0, p1, p2, p3, arrived, out, user_zero, user_scale, acc, users, base
):
    payloads = (p0, p1, p2, p3)
    tile_rows, share = arrived.shape[:2]
    step = users.shape[1]
    half = BS // 2
    u_dev = BS // share
    lane = lax.broadcasted_iota(jnp.int32, (step // 2, BS), 1)
    for row in range(tile_rows):
        here = jnp.zeros((step // 2, BS), F32)
        there = jnp.zeros((step // 2, BS), F32)
        for x in range(share):
            block = arrived[row, x].astype(F32)
            here = jnp.where(lane // u_dev == x, block, here)
            there = jnp.where(lane // u_dev == (x + share // 2) % share, block, there)
        there = pltpu.roll(there, half, 1)
        low = jnp.where(lane < half, here, there)
        high = jnp.where(lane < half, there, here)
        users[row] = jnp.concatenate([low, high], axis=0).astype(BF16)

    lane = lax.broadcasted_iota(jnp.int32, (step, BS), 1)
    zero = jnp.zeros((step, BS), F32)
    degree = jnp.ones((step, BS), F32)
    for away, payload in enumerate(payloads):
        x = lax.rem(place[1] + (share - away), share)
        values, extra = payload[place[1]], payload[share]
        base[x, 0], base[x, 1] = values, extra
        piece = values.astype(F32)[:, half : half + u_dev]
        zero = jnp.where(lane // u_dev == x, jnp.concatenate([piece] * share, axis=1), zero)
        piece = extra.astype(F32)[:, half : half + u_dev]
        degree = jnp.where(lane // u_dev == x, jnp.concatenate([piece] * share, axis=1), degree)
    user_zero[...] = zero
    user_scale[...] = lax.rsqrt(degree)

    item_products(place, slots, payloads, users, acc)
    tile_cols = acc.shape[1]
    for x in range(share):
        for col in range(tile_cols):
            out[x * tile_cols + col] = acc[x, col].astype(BF16)
    first_block = share * tile_cols
    for pair in range(share // 2):
        first, degree = (
            jnp.concatenate(
                [base[2 * pair + k, part].astype(F32)[:, :half] for k in range(2)], axis=1
            )
            for part in range(2)
        )
        out[first_block + pair] = (lax.rsqrt(degree) * first).astype(BF16)
        out[first_block + share // 2 + pair] = degree.astype(BF16)


def users_kernel(place, slots, p0, p1, p2, p3, gathered, out, item_sum, acc, sent):
    share, tile_cols, step = item_sum.shape[:3]
    n_row = gathered.shape[0]
    half = BS // 2
    base = share * tile_cols

    def of_tile(block, x, col):
        pair, side = block + x // 2, (x % 2) * half
        return jnp.concatenate(
            [gathered[2 * col + k, pair].astype(F32)[:, side : side + half] for k in range(2)],
            axis=1,
        )

    for x in range(share):
        for col in range(tile_cols):
            at = x * tile_cols + col
            total = gathered[0, at].astype(F32)
            for part in range(1, n_row):
                total = total + gathered[part, at].astype(F32)
            item_sum[x, col] = total
            scale = lax.rsqrt(of_tile(base + share // 2, x, col))
            sent[x, col, :step] = of_tile(base, x, col).astype(BF16)
            sent[x, col, step:] = (scale * (scale * total)).astype(BF16)
    acc[...] = jnp.zeros_like(acc)
    for x, row, col, live, tile in slot_list(place, slots, (p0, p1, p2, p3)):
        prod = lax.dot_general(
            sent[x, col], tile, (((1,), (1,)), ((), ())), preferred_element_type=F32
        )
        acc[row] += jnp.where(live, prod, 0.0)
    out[...] = acc[...].astype(BF16)


def users_sum_kernel(parts, user_zero, user_scale, message, user_final):
    step = message.shape[1]
    total = parts[0].astype(F32)
    for part in range(1, parts.shape[0]):
        total = total + parts[part].astype(F32)
    scale = user_scale[...]
    users_one = scale * total[:step]
    users_two = scale * total[step:]
    message[...] = jnp.broadcast_to((scale * users_one).astype(BF16)[None], message.shape)
    user_final[...] = (user_zero[...] + users_one + users_two) / 3.0


def items_two_kernel(
    place, slots, p0, p1, p2, p3, users, item_sum, user_final, out, acc
):
    item_products(place, slots, (p0, p1, p2, p3), users, acc)
    share, tile_cols, step = acc.shape[:3]
    n_row = 2 * tile_cols
    half = BS // 2
    u_dev = BS // share
    run, quarter = step // 2, step // 4
    for x in range(share):
        own = user_final[...][:, x * u_dev : (x + 1) * u_dev]
        own = jnp.concatenate(
            [own[p * quarter : (p + 1) * quarter, :] for p in range(4)], axis=1
        )
        for col in range(tile_cols):
            total = acc[x, col] + item_sum[x, col] * (1.0 / n_row)
            for k in range(2):
                side = total[:, k * half : (k + 1) * half]
                block = jnp.concatenate([side[:run, :], side[run:, :]], axis=1).astype(BF16)
                out[2 * col + k, x, 0] = block[:quarter, :]
                out[2 * col + k, x, 1] = block[quarter:, :]
                mine = place[0] == 2 * col + k
                out[2 * col + k, x, 2] = jnp.where(mine, own, 0.0).astype(BF16)


def final_kernel(arrived, payload, item_final, user_final):
    n_row, share = arrived.shape[:2]
    i_dev, emb = item_final.shape
    u_dev = user_final.shape[0]
    total = arrived[0].astype(F32)
    for part in range(1, n_row):
        total = total + arrived[part].astype(F32)
    run, quarter = emb // share // 2, emb // share // 4
    scale = lax.rsqrt(payload[share].astype(F32)[:1, :i_dev])
    scale = jnp.concatenate([scale, scale], axis=1)
    sums = jnp.concatenate([total[x, p] for x in range(share) for p in range(2)], axis=0)
    own = [payload[x].astype(F32)[:, :i_dev] for x in range(share)]
    own = [jnp.concatenate([one[:run], one[run:]], axis=1) for one in own]
    layers = (jnp.concatenate(own, axis=0) + scale * sums) / 3.0
    below = jnp.concatenate([total[x, 2] for x in range(share)], axis=0)
    pad = jnp.zeros((BS - sums.shape[0] - below.shape[0], BS), F32)
    both = jnp.concatenate([layers, below, pad], axis=0).T
    width = share * run
    layers = jnp.concatenate([both[:i_dev, :width], both[i_dev : 2 * i_dev, :width]], axis=1)
    item_final[...] = layers.astype(BF16)
    pieces = []
    for h in range(2):
        for x in range(share):
            for p in range(2):
                rows = slice((2 * h + p) * u_dev, (2 * h + p + 1) * u_dev)
                first = width + x * quarter
                pieces.append(both[rows, first : first + quarter])
    user_final[...] = jnp.concatenate(pieces, axis=1).astype(BF16)


def exchange(values, axes):
    return lax.all_to_all(values, axes, split_axis=0, concat_axis=0, tiled=True)


def per_device(
    user_emb, item_emb, user_degree, item_degree, block_values, block_row, block_col, block_count
):
    share = lax.axis_size("x")
    n_row = lax.axis_size(ROW)
    tile_rows = lax.axis_size(PLANE)
    n_col = tile_rows * share
    u_dev, emb = user_emb.shape
    i_dev = item_emb.shape[0]
    tile_cols = i_dev * n_row // BS
    step = emb // share
    shape = jax.ShapeDtypeStruct
    acc_items = pltpu.VMEM((share, tile_cols, step, BS), F32)

    item_degree = item_degree.reshape(1, i_dev)
    held = NBLK * BS // step
    payload, message = call(
        start_kernel,
        "start",
        (shape((share + 1 + held, step, BS), BF16), shape((tile_rows, share, step // 2, BS), BF16)),
        [HBM] * 8,
        [
            pltpu.VMEM((i_dev, emb), BF16),
            pltpu.VMEM((u_dev, emb), BF16),
            pltpu.VMEM((1, i_dev), jnp.int32),
            pltpu.VMEM((1, u_dev), jnp.int32),
            pltpu.VMEM((1, 1, NBLK), jnp.int32),
            pltpu.VMEM((1, 1, NBLK), jnp.int32),
            pltpu.VMEM((1, 1, 1), jnp.int32),
            pltpu.VMEM((held, step, BS), BF16),
            pltpu.VMEM((share + 1, step, BS), BF16),
            pltpu.SemaphoreType.DMA((10,)),
        ],
        (HBM, VMEM),
        vmem=60,
    )(
        item_emb, user_emb, item_degree, user_degree.reshape(1, u_dev), block_row, block_col,
        block_count.reshape(1, 1, 1), block_values.reshape(held, step, BS),
    )
    with jax.named_scope("sent_users_0"):
        arrived = exchange(message.reshape(n_col, step // 2, BS), PLANE + ("x",))
    with jax.named_scope("payloads_along_x"):
        payloads = [payload] + [
            lax.ppermute(payload, "x", [(x, (x + away) % share) for x in range(share)])
            for away in range(1, share)
        ]
    place = jnp.stack([lax.axis_index(ROW), lax.axis_index("x")]).astype(jnp.int32)
    first_slot = i_dev + u_dev
    slots = jnp.stack(
        [one[share, 0, first_slot : first_slot + 2 * NBLK + 1] for one in payloads]
    ).astype(jnp.int32)
    slotted = [SMEM] * 2 + [VMEM] * share
    slot_args = (place, slots, *payloads)
    blocks = share * tile_cols + share
    message, user_zero, user_scale = call(
        items_one_kernel,
        "items_1_parts",
        (shape((blocks, step, BS), BF16), shape((step, BS), F32), shape((step, BS), F32)),
        slotted + [VMEM],
        [
            acc_items,
            pltpu.VMEM((tile_rows, step, BS), BF16),
            pltpu.VMEM((share, 2, step, BS), BF16),
        ],
    )(*slot_args, arrived.reshape(tile_rows, share, step // 2, BS))
    with jax.named_scope("items_0_and_1"):
        gathered = lax.all_gather(message, ROW, axis=0)
    message, item_sum = call(
        users_kernel,
        "users_1_and_2_parts",
        (shape((tile_rows, 2 * step, BS), BF16), shape((share, tile_cols, step, BS), F32)),
        slotted + [VMEM],
        [
            pltpu.VMEM((tile_rows, 2 * step, BS), F32),
            pltpu.VMEM((share, tile_cols, 2 * step, BS), BF16),
        ],
    )(*slot_args, gathered)
    with jax.named_scope("users_1_and_2"):
        parts = exchange(message, PLANE)
    message, user_final = call(
        users_sum_kernel,
        "users_sum",
        (shape((tile_rows, step, BS), BF16), shape((step, BS), F32)),
        [VMEM] * 3,
    )(parts, user_zero, user_scale)
    with jax.named_scope("sent_users_1"):
        users = exchange(message, PLANE)
    message = call(
        items_two_kernel,
        "items_2_parts",
        shape((n_row, share, 3, step // 4, BS), BF16),
        slotted + [VMEM] * 3,
        [acc_items],
    )(*slot_args, users, item_sum, user_final)
    with jax.named_scope("items_2"):
        parts = exchange(message.reshape(n_row * share, *message.shape[2:]), ROW + ("x",))
    item_final, user_final = call(
        final_kernel,
        "final",
        (shape((i_dev, emb), BF16), shape((u_dev, emb), BF16)),
        [VMEM, VMEM],
    )(parts.reshape(message.shape), payload)
    return user_final, item_final


def solution(mesh):
    fine = Mesh(mesh.devices.reshape(4, 2, 4, 8, 4), AXES)
    col = PLANE + ("x",)
    in_specs = (
        P(AXES, None),
        P(AXES, None),
        P(AXES),
        P(AXES),
        P(ROW, col, None, None, None),
        P(ROW, col, None),
        P(ROW, col, None),
        P(ROW, col),
    )
    out_specs = (P(AXES, None), P(AXES, None))
    return jax.shard_map(
        per_device, mesh=fine, in_specs=in_specs, out_specs=out_specs, check_vma=False
    )
```

time: 141 us -> 136 us (0.965)
  waiting for transfers between devices: 25.6 us -> 11.9 us
  blocking collectives: 79.5 us -> 87.9 us
    all_to_all x2 -> x1, waiting for transfers between devices: 25.6 us -> 11.9 us  [exchange(): return lax.all_to_all(values, axes, split_axis=0, concat_axis=0, tiled=True)]
    all_to_all x3, blocking collectives: 43.7 us -> 56.3 us  [exchange(): return lax.all_to_all(values, axes, split_axis=0, concat_axis=0, tiled=True)]
    ppermute x0 -> x3, starting transfers between devices: none -> 10.3 us  [per_device(): lax.ppermute(payload, 'x', [(x, (x + away) % share) for x in range(share)])]
    all_to_all x2 -> x1, starting transfers between devices: 26.2 us -> 16.3 us  [exchange(): return lax.all_to_all(values, axes, split_axis=0, concat_axis=0, tiled=True)]
    all_gather x1, blocking collectives: 35.7 us -> 31.6 us  [per_device(): gathered = lax.all_gather(message, ROW, axis=0)]
    pallas_call x4 -> x3, Pallas kernels: 6.01 us -> 4.77 us  [the longest x1 2.63 us: per_device(): call(start_kernel, 'start', (shape((share + 1 + held, step, BS), BF16), s...]
  transfers between devices with their start and end apart: 2 -> 4, of which waited for: 2 -> 1; matrix products, arithmetic and copies ran while one was open for 0% -> 0% of each run, Pallas kernels for 0% -> 0%
where the time goes in v4:
time: 136 us; the launch traced here: 135 us
  blocking collectives  87.9 us (65%)
  starting transfers between devices  26.6 us (20%)
  waiting for transfers between devices  11.9 us (9%)
  Pallas kernels  7.05 us (5%)
  between operations  1.37 us (1%)
    all_to_all x3, blocking collectives, exchange(): return lax.all_to_all(values, axes, split_axis=0, concat_axis=0, tiled=True)  56.3 us
    all_gather x1, blocking collectives, per_device(): gathered = lax.all_gather(message, ROW, axis=0)  31.6 us
    all_to_all x1, starting transfers between devices, exchange(): return lax.all_to_all(values, axes, split_axis=0, concat_axis=0, tiled=True)  16.3 us
    all_to_all x1, waiting for transfers between devices, exchange(): return lax.all_to_all(values, axes, split_axis=0, concat_axis=0, tiled=True)  11.9 us
    ppermute x3, starting transfers between devices, per_device(): lax.ppermute(payload, 'x', [(x, (x + away) % share) for x in range(share)])  10.3 us
  transfers between devices with their start and end apart: 4, of which 1 were waited for; matrix products, arithmetic and copies ran while one was open for 0% of the time, Pallas kernels for 0%

profile of v4, /device:TPU:1, one launch (start us, length us, event | category | flops | bytes accessed | tf_op | source)
XLA Modules:
  0.0 135.2 jit_solution(9769188253832997929)
XLA Ops:
  1.3 2.6 %start.1 = (bf16[69,16,128]{2,1,0:T(8,128)(2,1)}, bf16[32,4,8,128]{3,2,1,0:T(8,128)(2,1)}) custom-call(bf16[64,64]{1,0:T(8,128)(2,1)} %item_emb.1, bf16[32,64]{1,0:T(8,128)(2,1)} %user_emb.1, s32[1,64]{1,0:T(1,128)} %bitcast.26, s32[1,32]{1,0:T(1,128)} %bitcast.27, s32[1,1,8]{2,1,0:T(1,128)} %rows.1, s32[1,1,8]{2,1,0:T(1,128)} %cols.1, ...), custom_call_target="tpu_custom_call" | custom-call | tf_op jit(solution)/shard_map/start/pallas_call | solution.py:302
  3.9 0.0 copy-start
  3.9 5.3 %collective-permute-start.2 = (bf16[69,16,128]{2,1,0:T(8,128)(2,1)}, bf16[69,16,128]{2,1,0:T(8,128)(2,1)S(1)}, u32[]{:S(2)}, u32[]{:S(2)}) collective-permute-start(bf16[69,16,128]{2,1,0:T(8,128)(2,1)} %get-tuple-element.13.p0.payload), channel_id=1, source_target_pairs={{0,3},{1,0},{2,1},{3,2},{4,7},{5,4},{6,5},{7,6},{8,11},{9,8},{10,9... | collective-permute-start | bytes 847880 | tf_op jit(solution)/shard_map/payloads_along_x/ppermute | solution.py:329
  9.3 2.4 %collective-permute-start.1 = (bf16[69,16,128]{2,1,0:T(8,128)(2,1)}, bf16[69,16,128]{2,1,0:T(8,128)(2,1)S(1)}, u32[]{:S(2)}, u32[]{:S(2)}) collective-permute-start(bf16[69,16,128]{2,1,0:T(8,128)(2,1)} %get-tuple-element.13.p0.payload), channel_id=1, source_target_pairs={{0,2},{1,3},{2,0},{3,1},{4,6},{5,7},{6,4},{7,5},{8,10},{9,11},{10,... | collective-permute-start | bytes 847880 | tf_op jit(solution)/shard_map/payloads_along_x/ppermute | solution.py:329
  11.7 2.5 %collective-permute-start = (bf16[69,16,128]{2,1,0:T(8,128)(2,1)}, bf16[69,16,128]{2,1,0:T(8,128)(2,1)S(1)}, u32[]{:S(2)}, u32[]{:S(2)}) collective-permute-start(bf16[69,16,128]{2,1,0:T(8,128)(2,1)} %get-tuple-element.13.p0.payload), channel_id=1, source_target_pairs={{0,1},{1,2},{2,3},{3,0},{4,5},{5,6},{6,7},{7,4},{8,9},{9,10},{10,1... | collective-permute-start | bytes 847880 | tf_op jit(solution)/shard_map/payloads_along_x/ppermute | solution.py:329
  14.2 16.3 %all-to-all-start = ((bf16[128,8,128]{2,1,0:T(8,128)(2,1)}), bf16[128,8,128]{2,1,0:T(8,128)(2,1)S(1)}, u32[]{:S(2)}, u32[]{:S(2)}) async-start(bf16[128,8,128]{2,1,0:T(8,128)(2,1)} %bitcast.25), calls=%async_computation | async-start | bytes 524288 | tf_op jit(solution)/shard_map/sent_users_0/all_to_all | solution.py:283
  30.5 0.0 copy-done
  30.5 0.1 slice_bitcast_fusion.3
  30.6 0.1 pad_add_fusion.place
  30.7 0.0 collective-permute-done.2.p3
  30.7 0.1 slice_bitcast_fusion
  30.8 0.0 collective-permute-done.1.p2
  30.8 0.1 slice_bitcast_fusion.1
  30.8 0.0 collective-permute-done.p1
  30.8 0.1 slice_bitcast_fusion.2
  30.9 11.9 %all-to-all-done = bf16[128,8,128]{2,1,0:T(8,128)(2,1)S(1)} async-done(((bf16[128,8,128]{2,1,0:T(8,128)(2,1)}), bf16[128,8,128]{2,1,0:T(8,128)(2,1)S(1)}, u32[]{:S(2)}, u32[]{:S(2)}) %all-to-all-start) | async-done | bytes 262176 | tf_op jit(solution)/shard_map/sent_users_0/all_to_all | solution.py:283
  42.8 1.1 items_1_parts.1
  43.9 31.6 %all-gather = bf16[160,16,128]{2,1,0:T(8,128)(2,1)S(1)} all-gather(bf16[20,16,128]{2,1,0:T(8,128)(2,1)S(1)} %get-tuple-element.15), channel_id=2, replica_groups=mesh['zh'=4,'co'=2,'zl'=4,'y'=8,'x'=4] {'zh','co'}, dimensions={0}, use_global_device_ids=true | all-gather | bytes 737280 | tf_op jit(solution)/shard_map/items_0_and_1/all_gather | solution.py:352
  75.5 1.3 users_1_and_2_parts.1
  76.9 16.7 %all_to_all.20.parts = bf16[32,32,128]{2,1,0:T(8,128)(2,1)S(1)} all-to-all(bf16[32,32,128]{2,1,0:T(8,128)(2,1)S(1)} %get-tuple-element.16), channel_id=1, replica_groups=mesh['zh'=4,'co'=2,'zl'=4,'y'=8,'x'=4] {'zl','y'}, dimensions={0} | all-to-all | bytes 524288 | tf_op jit(solution)/shard_map/users_1_and_2/all_to_all | solution.py:283
  93.5 0.1 users_sum.1
  93.6 14.3 %all_to_all.21.users = bf16[32,16,128]{2,1,0:T(8,128)(2,1)S(1)} all-to-all(bf16[32,16,128]{2,1,0:T(8,128)(2,1)S(1)} %get-tuple-element.19), channel_id=1, replica_groups=mesh['zh'=4,'co'=2,'zl'=4,'y'=8,'x'=4] {'zl','y'}, dimensions={0} | all-to-all | bytes 262144 | tf_op jit(solution)/shard_map/sent_users_1/all_to_all | solution.py:283
  107.9 1.1 items_2_parts.1
  109.0 25.3 %all_to_all.22 = bf16[32,3,4,128]{3,2,1,0:T(4,128)(2,1)S(1)} all-to-all(bf16[32,3,4,128]{3,2,1,0:T(4,128)(2,1)S(1)} %bitcast.23), channel_id=1, replica_groups=mesh['zh'=4,'co'=2,'zl'=4,'y'=8,'x'=4] {'zh','co','x'}, dimensions={0} | all-to-all | bytes 196608 | tf_op jit(solution)/shard_map/items_2/all_to_all | solution.py:283
  134.3 0.9 final.1
  (1 shorter events, 0.0 us)
Async XLA Ops:
  3.9 26.6 %copy-start = (bf16[69,16,128]{2,1,0:T(8,128)(2,1)S(1)}, bf16[69,16,128]{2,1,0:T(8,128)(2,1)}, u32[]{:S(2)}) copy-start(bf16[69,16,128]{2,1,0:T(8,128)(2,1)} %get-tuple-element.13.p0.payload) | copy-start | bytes 847876
  3.9 26.8 %collective-permute-start.2 = (bf16[69,16,128]{2,1,0:T(8,128)(2,1)}, bf16[69,16,128]{2,1,0:T(8,128)(2,1)S(1)}, u32[]{:S(2)}, u32[]{:S(2)}) collective-permute-start(bf16[69,16,128]{2,1,0:T(8,128)(2,1)} %get-tuple-element.13.p0.payload), channel_id=1, source_target_pairs={{0,3},{1,0},{2,1},{3,2},{4,7},{5,4},{6,5},{7,6},{8,11},{9,8},{10,9... | collective-permute-start | bytes 847880 | tf_op jit(solution)/shard_map/payloads_along_x/ppermute | solution.py:329
  9.3 21.5 %collective-permute-start.1 = (bf16[69,16,128]{2,1,0:T(8,128)(2,1)}, bf16[69,16,128]{2,1,0:T(8,128)(2,1)S(1)}, u32[]{:S(2)}, u32[]{:S(2)}) collective-permute-start(bf16[69,16,128]{2,1,0:T(8,128)(2,1)} %get-tuple-element.13.p0.payload), channel_id=1, source_target_pairs={{0,2},{1,3},{2,0},{3,1},{4,6},{5,7},{6,4},{7,5},{8,10},{9,11},{10,... | collective-permute-start | bytes 847880 | tf_op jit(solution)/shard_map/payloads_along_x/ppermute | solution.py:329
  11.7 19.1 %collective-permute-start = (bf16[69,16,128]{2,1,0:T(8,128)(2,1)}, bf16[69,16,128]{2,1,0:T(8,128)(2,1)S(1)}, u32[]{:S(2)}, u32[]{:S(2)}) collective-permute-start(bf16[69,16,128]{2,1,0:T(8,128)(2,1)} %get-tuple-element.13.p0.payload), channel_id=1, source_target_pairs={{0,1},{1,2},{2,3},{3,0},{4,5},{5,6},{6,7},{7,4},{8,9},{9,10},{10,1... | collective-permute-start | bytes 847880 | tf_op jit(solution)/shard_map/payloads_along_x/ppermute | solution.py:329
  14.2 28.6 %all-to-all-start = ((bf16[128,8,128]{2,1,0:T(8,128)(2,1)}), bf16[128,8,128]{2,1,0:T(8,128)(2,1)S(1)}, u32[]{:S(2)}, u32[]{:S(2)}) async-start(bf16[128,8,128]{2,1,0:T(8,128)(2,1)} %bitcast.25), calls=%async_computation | async-start | bytes 524288 | tf_op jit(solution)/shard_map/sent_users_0/all_to_all | solution.py:283

commit v5 on v4

--- a/solution.py
+++ b/solution.py
@@ -48,7 +48,7 @@
 
 def start_kernel(
     item_emb, user_emb, item_degree, user_degree, rows, cols, count, tiles, payload, message,
-    items, users, item_deg, user_deg, slot_rows, slot_cols, live, held, base, sems,
+    items, users, item_deg, user_deg, slot_rows, slot_cols, live, held, base, sent_users, sems,
 ):
     share = message.shape[1]
     i_dev, emb = item_emb.shape
@@ -65,6 +65,8 @@
     ]
     (fetched,) = fetch([(tiles, held)], sems, len(small))
     ready = fetch(small, sems, 0)
+    fetched.wait()
+    outgoing = fetch([(held, payload.at[pl.ds(share + 1, held.shape[0])])], sems, len(small) + 1)
     for copy in ready:
         copy.wait()
     values = jnp.concatenate(
@@ -81,7 +83,7 @@
             user_deg[...],
             slot_rows[0],
             slot_cols[0],
-            live[0],
+            live[...].reshape(1, 1),
             jnp.zeros((1, BS - i_dev - u_dev - 2 * NBLK - 1), jnp.int32),
         ],
         axis=1,
@@ -92,19 +94,15 @@
         columns = columns_of(values, to, step)
         base[to] = columns.astype(BF16)
         sent = scale * columns[:, i_dev : i_dev + u_dev]
-        low, high = sent[: step // 2], sent[step // 2 :]
-        block = jnp.concatenate([low, low, high, high], axis=1).astype(BF16)
-        message[:, to] = jnp.broadcast_to(block[None], (message.shape[0], *block.shape))
-    fetched.wait()
-    last = fetch(
-        [
-            (base, payload.at[pl.ds(0, share + 1)]),
-            (held, payload.at[pl.ds(share + 1, held.shape[0])]),
-        ],
-        sems,
-        len(small) + 1,
+        quarter = message.shape[2]
+        block = jnp.concatenate(
+            [sent[p * quarter : (p + 1) * quarter, :] for p in range(share)], axis=1
+        ).astype(BF16)
+        sent_users[:, to] = jnp.broadcast_to(block[None], (message.shape[0], *block.shape))
+    outgoing += fetch(
+        [(base, payload.at[pl.ds(0, share + 1)]), (sent_users, message)], sems, len(small) + 2
     )
-    for copy in last:
+    for copy in outgoing:
         copy.wait()
 
 
@@ -136,18 +134,23 @@
     step = users.shape[1]
     half = BS // 2
     u_dev = BS // share
-    lane = lax.broadcasted_iota(jnp.int32, (step // 2, BS), 1)
+    quarter = arrived.shape[2]
+    group = lax.broadcasted_iota(jnp.int32, (quarter, BS), 1) // u_dev
     for row in range(tile_rows):
-        here = jnp.zeros((step // 2, BS), F32)
-        there = jnp.zeros((step // 2, BS), F32)
-        for x in range(share):
-            block = arrived[row, x].astype(F32)
-            here = jnp.where(lane // u_dev == x, block, here)
-            there = jnp.where(lane // u_dev == (x + share // 2) % share, block, there)
-        there = pltpu.roll(there, half, 1)
-        low = jnp.where(lane < half, here, there)
-        high = jnp.where(lane < half, there, here)
-        users[row] = jnp.concatenate([low, high], axis=0).astype(BF16)
+        blocks = [arrived[row, x].astype(F32) for x in range(share)]
+        turned = []
+        for away in range(share):
+            mixed = blocks[0]
+            for x in range(1, share):
+                mixed = jnp.where(group == (x - away) % share, blocks[x], mixed)
+            turned.append(pltpu.roll(mixed, away * u_dev, 1) if away else mixed)
+        parts = []
+        for p in range(share):
+            part = turned[-p % share]
+            for x in range(1, share):
+                part = jnp.where(group == x, turned[(x - p) % share], part)
+            parts.append(part)
+        users[row] = jnp.concatenate(parts, axis=0).astype(BF16)
 
     lane = lax.broadcasted_iota(jnp.int32, (step, BS), 1)
     zero = jnp.zeros((step, BS), F32)
@@ -302,7 +305,7 @@
     payload, message = call(
         start_kernel,
         "start",
-        (shape((share + 1 + held, step, BS), BF16), shape((tile_rows, share, step // 2, BS), BF16)),
+        (shape((share + 1 + held, step, BS), BF16), shape((tile_rows, share, step // share, BS), BF16)),
         [HBM] * 8,
         [
             pltpu.VMEM((i_dev, emb), BF16),
@@ -311,19 +314,20 @@
             pltpu.VMEM((1, u_dev), jnp.int32),
             pltpu.VMEM((1, 1, NBLK), jnp.int32),
             pltpu.VMEM((1, 1, NBLK), jnp.int32),
-            pltpu.VMEM((1, 1, 1), jnp.int32),
+            pltpu.VMEM((1,), jnp.int32),
             pltpu.VMEM((held, step, BS), BF16),
             pltpu.VMEM((share + 1, step, BS), BF16),
-            pltpu.SemaphoreType.DMA((10,)),
+            pltpu.VMEM((tile_rows, share, step // share, BS), BF16),
+            pltpu.SemaphoreType.DMA((11,)),
         ],
-        (HBM, VMEM),
+        (HBM, HBM),
         vmem=60,
     )(
         item_emb, user_emb, item_degree, user_degree.reshape(1, u_dev), block_row, block_col,
-        block_count.reshape(1, 1, 1), block_values.reshape(held, step, BS),
+        block_count.reshape(1), block_values.reshape(held, step, BS),
     )
     with jax.named_scope("sent_users_0"):
-        arrived = exchange(message.reshape(n_col, step // 2, BS), PLANE + ("x",))
+        arrived = exchange(message.reshape(n_col, step // share, BS), PLANE + ("x",))
     with jax.named_scope("payloads_along_x"):
         payloads = [payload] + [
             lax.ppermute(payload, "x", [(x, (x + away) % share) for x in range(share)])
@@ -337,6 +341,7 @@
     slotted = [SMEM] * 2 + [VMEM] * share
     slot_args = (place, slots, *payloads)
     blocks = share * tile_cols + share
+    first_shape = message.shape
     message, user_zero, user_scale = call(
         items_one_kernel,
         "items_1_parts",
@@ -347,7 +352,7 @@
             pltpu.VMEM((tile_rows, step, BS), BF16),
             pltpu.VMEM((share, 2, step, BS), BF16),
         ],
-    )(*slot_args, arrived.reshape(tile_rows, share, step // 2, BS))
+    )(*slot_args, arrived.reshape(first_shape))
     with jax.named_scope("items_0_and_1"):
         gathered = lax.all_gather(message, ROW, axis=0)
     message, item_sum = call(

time: 136 us -> 133 us (0.978)
    all_to_all x3, blocking collectives: 56.3 us -> 52.9 us  [exchange(): return lax.all_to_all(values, axes, split_axis=0, concat_axis=0, tiled=True)]
    all_gather x1, blocking collectives: 31.6 us -> 34 us  [per_device(): gathered = lax.all_gather(message, ROW, axis=0)]
where the time goes in v5:
time: 133 us
  blocking collectives  86.9 us (65%)
  starting transfers between devices  26.6 us (20%)
  waiting for transfers between devices  11 us (8%)
  Pallas kernels  6.48 us (5%)
  between operations  1.37 us (1%)
    all_to_all x3, blocking collectives, exchange(): return lax.all_to_all(values, axes, split_axis=0, concat_axis=0, tiled=True)  52.9 us
    all_gather x1, blocking collectives, per_device(): gathered = lax.all_gather(message, ROW, axis=0)  34 us
    all_to_all x1, starting transfers between devices, exchange(): return lax.all_to_all(values, axes, split_axis=0, concat_axis=0, tiled=True)  16.3 us
    all_to_all x1, waiting for transfers between devices, exchange(): return lax.all_to_all(values, axes, split_axis=0, concat_axis=0, tiled=True)  10.9 us
    ppermute x3, starting transfers between devices, per_device(): lax.ppermute(payload, 'x', [(x, (x + away) % share) for x in range(share)])  10.3 us
  transfers between devices with their start and end apart: 4, of which 1 were waited for; matrix products, arithmetic and copies ran while one was open for 0% of the time, Pallas kernels for 0%

profile of v5, /device:TPU:1, one launch (start us, length us, event | category | flops | bytes accessed | tf_op | source)
XLA Modules:
  0.0 132.6 jit_solution(13675197095114004563)
XLA Ops:
  1.3 2.0 %start.1 = (bf16[69,16,128]{2,1,0:T(8,128)(2,1)}, bf16[32,4,4,128]{3,2,1,0:T(4,128)(2,1)}) custom-call(bf16[64,64]{1,0:T(8,128)(2,1)} %item_emb.1, bf16[32,64]{1,0:T(8,128)(2,1)} %user_emb.1, s32[1,64]{1,0:T(1,128)} %bitcast.26, s32[1,32]{1,0:T(1,128)} %bitcast.27, s32[1,1,8]{2,1,0:T(1,128)} %rows.1, s32[1,1,8]{2,1,0:T(1,128)} %cols.1, s32[1]{0:T(128)} %bitcast.19.count, ...), custom_call_target="tpu_custom_call" | custom-call | tf_op jit(solution)/shard_map/start/pallas_call | solution.py:305
  3.3 0.0 copy-start
  3.3 5.3 %collective-permute-start.2 = (bf16[69,16,128]{2,1,0:T(8,128)(2,1)}, bf16[69,16,128]{2,1,0:T(8,128)(2,1)S(1)}, u32[]{:S(2)}, u32[]{:S(2)}) collective-permute-start(bf16[69,16,128]{2,1,0:T(8,128)(2,1)} %get-tuple-element.13.p0.payload), channel_id=1, source_target_pairs={{0,3},{1,0},{2,1},{3,2},{4,7},{5,4},{6,5},{7,6},{8,11},{9,8},{10,9... | collective-permute-start | bytes 847880 | tf_op jit(solution)/shard_map/payloads_along_x/ppermute | solution.py:333
  8.6 2.4 %collective-permute-start.1 = (bf16[69,16,128]{2,1,0:T(8,128)(2,1)}, bf16[69,16,128]{2,1,0:T(8,128)(2,1)S(1)}, u32[]{:S(2)}, u32[]{:S(2)}) collective-permute-start(bf16[69,16,128]{2,1,0:T(8,128)(2,1)} %get-tuple-element.13.p0.payload), channel_id=1, source_target_pairs={{0,2},{1,3},{2,0},{3,1},{4,6},{5,7},{6,4},{7,5},{8,10},{9,11},{10,... | collective-permute-start | bytes 847880 | tf_op jit(solution)/shard_map/payloads_along_x/ppermute | solution.py:333
  11.1 2.5 %collective-permute-start = (bf16[69,16,128]{2,1,0:T(8,128)(2,1)}, bf16[69,16,128]{2,1,0:T(8,128)(2,1)S(1)}, u32[]{:S(2)}, u32[]{:S(2)}) collective-permute-start(bf16[69,16,128]{2,1,0:T(8,128)(2,1)} %get-tuple-element.13.p0.payload), channel_id=1, source_target_pairs={{0,1},{1,2},{2,3},{3,0},{4,5},{5,6},{6,7},{7,4},{8,9},{9,10},{10,1... | collective-permute-start | bytes 847880 | tf_op jit(solution)/shard_map/payloads_along_x/ppermute | solution.py:333
  13.6 16.3 %all-to-all-start = ((bf16[128,4,128]{2,1,0:T(4,128)(2,1)}), bf16[128,4,128]{2,1,0:T(4,128)(2,1)S(1)}, u32[]{:S(2)}, u32[]{:S(2)}) async-start(bf16[128,4,128]{2,1,0:T(4,128)(2,1)} %bitcast.25), calls=%async_computation | async-start | bytes 262144 | tf_op jit(solution)/shard_map/sent_users_0/all_to_all | solution.py:286
  29.9 0.0 copy-done
  29.9 0.1 slice_bitcast_fusion.3
  30.0 0.1 pad_add_fusion.place
  30.0 0.0 collective-permute-done.2.p3
  30.0 0.1 slice_bitcast_fusion
  30.1 0.0 collective-permute-done.1.p2
  30.1 0.1 slice_bitcast_fusion.1
  30.2 0.0 collective-permute-done.p1
  30.2 0.1 slice_bitcast_fusion.2
  30.3 10.9 %all-to-all-done = bf16[128,4,128]{2,1,0:T(4,128)(2,1)S(1)} async-done(((bf16[128,4,128]{2,1,0:T(4,128)(2,1)}), bf16[128,4,128]{2,1,0:T(4,128)(2,1)S(1)}, u32[]{:S(2)}, u32[]{:S(2)}) %all-to-all-start) | async-done | bytes 131104 | tf_op jit(solution)/shard_map/sent_users_0/all_to_all | solution.py:286
  41.2 1.1 items_1_parts.1
  42.4 34.0 %all-gather = bf16[160,16,128]{2,1,0:T(8,128)(2,1)S(1)} all-gather(bf16[20,16,128]{2,1,0:T(8,128)(2,1)S(1)} %get-tuple-element.15), channel_id=2, replica_groups=mesh['zh'=4,'co'=2,'zl'=4,'y'=8,'x'=4] {'zh','co'}, dimensions={0}, use_global_device_ids=true | all-gather | bytes 737280 | tf_op jit(solution)/shard_map/items_0_and_1/all_gather | solution.py:357
  76.4 1.3 %users_1_and_2_parts.1 = (bf16[32,32,128]{2,1,0:T(8,128)(2,1)S(1)}, f32[4,4,16,128]{3,2,1,0:T(8,128)S(1)}) custom-call(s32[2]{0:T(128)S(1)} %pad_add_fusion.place, s32[4,17]{1,0:T(4,128)S(1)} %maximum_convert_fusion.slots, bf16[69,16,128]{2,1,0:T(8,128)(2,1)S(1)} %copy-done, bf16[69,16,128]{2,1,0:T(8,128)(2,1)S(1)} %collective-permute-done.p1, ...), custom_call_target="tpu_custom_call" | custom-call | tf_op jit(solution)/shard_map/users_1_and_2_parts/pallas_call | solution.py:358
  77.7 14.8 %all_to_all.20.parts = bf16[32,32,128]{2,1,0:T(8,128)(2,1)S(1)} all-to-all(bf16[32,32,128]{2,1,0:T(8,128)(2,1)S(1)} %get-tuple-element.16), channel_id=1, replica_groups=mesh['zh'=4,'co'=2,'zl'=4,'y'=8,'x'=4] {'zl','y'}, dimensions={0} | all-to-all | bytes 524288 | tf_op jit(solution)/shard_map/users_1_and_2/all_to_all | solution.py:286
  92.5 0.1 users_sum.1
  92.6 14.1 %all_to_all.21.users = bf16[32,16,128]{2,1,0:T(8,128)(2,1)S(1)} all-to-all(bf16[32,16,128]{2,1,0:T(8,128)(2,1)S(1)} %get-tuple-element.19), channel_id=1, replica_groups=mesh['zh'=4,'co'=2,'zl'=4,'y'=8,'x'=4] {'zl','y'}, dimensions={0} | all-to-all | bytes 262144 | tf_op jit(solution)/shard_map/sent_users_1/all_to_all | solution.py:286
  106.7 1.1 items_2_parts.1
  107.8 23.9 %all_to_all.22 = bf16[32,3,4,128]{3,2,1,0:T(4,128)(2,1)S(1)} all-to-all(bf16[32,3,4,128]{3,2,1,0:T(4,128)(2,1)S(1)} %bitcast.23), channel_id=1, replica_groups=mesh['zh'=4,'co'=2,'zl'=4,'y'=8,'x'=4] {'zh','co','x'}, dimensions={0} | all-to-all | bytes 196608 | tf_op jit(solution)/shard_map/items_2/all_to_all | solution.py:286
  131.7 0.9 final.1
  (1 shorter events, 0.0 us)
Async XLA Ops:
  3.3 26.6 %copy-start = (bf16[69,16,128]{2,1,0:T(8,128)(2,1)S(1)}, bf16[69,16,128]{2,1,0:T(8,128)(2,1)}, u32[]{:S(2)}) copy-start(bf16[69,16,128]{2,1,0:T(8,128)(2,1)} %get-tuple-element.13.p0.payload) | copy-start | bytes 847876
  3.3 26.8 %collective-permute-start.2 = (bf16[69,16,128]{2,1,0:T(8,128)(2,1)}, bf16[69,16,128]{2,1,0:T(8,128)(2,1)S(1)}, u32[]{:S(2)}, u32[]{:S(2)}) collective-permute-start(bf16[69,16,128]{2,1,0:T(8,128)(2,1)} %get-tuple-element.13.p0.payload), channel_id=1, source_target_pairs={{0,3},{1,0},{2,1},{3,2},{4,7},{5,4},{6,5},{7,6},{8,11},{9,8},{10,9... | collective-permute-start | bytes 847880 | tf_op jit(solution)/shard_map/payloads_along_x/ppermute | solution.py:333
  8.6 21.5 %collective-permute-start.1 = (bf16[69,16,128]{2,1,0:T(8,128)(2,1)}, bf16[69,16,128]{2,1,0:T(8,128)(2,1)S(1)}, u32[]{:S(2)}, u32[]{:S(2)}) collective-permute-start(bf16[69,16,128]{2,1,0:T(8,128)(2,1)} %get-tuple-element.13.p0.payload), channel_id=1, source_target_pairs={{0,2},{1,3},{2,0},{3,1},{4,6},{5,7},{6,4},{7,5},{8,10},{9,11},{10,... | collective-permute-start | bytes 847880 | tf_op jit(solution)/shard_map/payloads_along_x/ppermute | solution.py:333
  11.1 19.1 %collective-permute-start = (bf16[69,16,128]{2,1,0:T(8,128)(2,1)}, bf16[69,16,128]{2,1,0:T(8,128)(2,1)S(1)}, u32[]{:S(2)}, u32[]{:S(2)}) collective-permute-start(bf16[69,16,128]{2,1,0:T(8,128)(2,1)} %get-tuple-element.13.p0.payload), channel_id=1, source_target_pairs={{0,1},{1,2},{2,3},{3,0},{4,5},{5,6},{6,7},{7,4},{8,9},{9,10},{10,1... | collective-permute-start | bytes 847880 | tf_op jit(solution)/shard_map/payloads_along_x/ppermute | solution.py:333
  13.6 27.6 %all-to-all-start = ((bf16[128,4,128]{2,1,0:T(4,128)(2,1)}), bf16[128,4,128]{2,1,0:T(4,128)(2,1)S(1)}, u32[]{:S(2)}, u32[]{:S(2)}) async-start(bf16[128,4,128]{2,1,0:T(4,128)(2,1)} %bitcast.25), calls=%async_computation | async-start | bytes 262144 | tf_op jit(solution)/shard_map/sent_users_0/all_to_all | solution.py:286

commit v6 on v5

--- a/solution.py
+++ b/solution.py
@@ -109,7 +109,7 @@
 def slot_list(place, slots, payloads):
     share = len(payloads)
     for away, payload in enumerate(payloads):
-        x = lax.rem(place[1] + (share - away), share)
+        x = lax.bitwise_xor(place[1], away)
         step = payload.shape[1]
         blocks = BS // step
         for slot in range(NBLK):
@@ -156,7 +156,7 @@
     zero = jnp.zeros((step, BS), F32)
     degree = jnp.ones((step, BS), F32)
     for away, payload in enumerate(payloads):
-        x = lax.rem(place[1] + (share - away), share)
+        x = lax.bitwise_xor(place[1], away)
         values, extra = payload[place[1]], payload[share]
         base[x, 0], base[x, 1] = values, extra
         piece = values.astype(F32)[:, half : half + u_dev]
@@ -246,19 +246,19 @@
             for k in range(2):
                 side = total[:, k * half : (k + 1) * half]
                 block = jnp.concatenate([side[:run, :], side[run:, :]], axis=1).astype(BF16)
-                out[2 * col + k, x, 0] = block[:quarter, :]
-                out[2 * col + k, x, 1] = block[quarter:, :]
+                out[x, 2 * col + k, 0] = block[:quarter, :]
+                out[x, 2 * col + k, 1] = block[quarter:, :]
                 mine = place[0] == 2 * col + k
-                out[2 * col + k, x, 2] = jnp.where(mine, own, 0.0).astype(BF16)
+                out[x, 2 * col + k, 2] = jnp.where(mine, own, 0.0).astype(BF16)
 
 
 def final_kernel(arrived, payload, item_final, user_final):
-    n_row, share = arrived.shape[:2]
+    share, n_row = arrived.shape[:2]
     i_dev, emb = item_final.shape
     u_dev = user_final.shape[0]
-    total = arrived[0].astype(F32)
+    total = arrived[:, 0].astype(F32)
     for part in range(1, n_row):
-        total = total + arrived[part].astype(F32)
+        total = total + arrived[:, part].astype(F32)
     run, quarter = emb // share // 2, emb // share // 4
     scale = lax.rsqrt(payload[share].astype(F32)[:1, :i_dev])
     scale = jnp.concatenate([scale, scale], axis=1)
@@ -330,7 +330,7 @@
         arrived = exchange(message.reshape(n_col, step // share, BS), PLANE + ("x",))
     with jax.named_scope("payloads_along_x"):
         payloads = [payload] + [
-            lax.ppermute(payload, "x", [(x, (x + away) % share) for x in range(share)])
+            lax.ppermute(payload, "x", [(x, x ^ away) for x in range(share)])
             for away in range(1, share)
         ]
     place = jnp.stack([lax.axis_index(ROW), lax.axis_index("x")]).astype(jnp.int32)
@@ -378,12 +378,12 @@
     message = call(
         items_two_kernel,
         "items_2_parts",
-        shape((n_row, share, 3, step // 4, BS), BF16),
+        shape((share, n_row, 3, step // 4, BS), BF16),
         slotted + [VMEM] * 3,
         [acc_items],
     )(*slot_args, users, item_sum, user_final)
     with jax.named_scope("items_2"):
-        parts = exchange(message.reshape(n_row * share, *message.shape[2:]), ROW + ("x",))
+        parts = exchange(message.reshape(n_row * share, *message.shape[2:]), ("x",) + ROW)
     item_final, user_final = call(
         final_kernel,
         "final",

time: 133 us -> 134 us (level)
  no operation moved by 1% of the time
where the time goes in v6:
time: 134 us; the launch traced here: 133 us
  blocking collectives  87.1 us (65%)
  starting transfers between devices  26.9 us (20%)
  waiting for transfers between devices  10.9 us (8%)
  Pallas kernels  6.46 us (5%)
  between operations  1.37 us (1%)
    all_to_all x3, blocking collectives, exchange(): return lax.all_to_all(values, axes, split_axis=0, concat_axis=0, tiled=True)  53.1 us
    all_gather x1, blocking collectives, per_device(): gathered = lax.all_gather(message, ROW, axis=0)  34 us
    all_to_all x1, starting transfers between devices, exchange(): return lax.all_to_all(values, axes, split_axis=0, concat_axis=0, tiled=True)  17.1 us
    all_to_all x1, waiting for transfers between devices, exchange(): return lax.all_to_all(values, axes, split_axis=0, concat_axis=0, tiled=True)  10.9 us
    ppermute x3, starting transfers between devices, per_device(): lax.ppermute(payload, 'x', [(x, x ^ away) for x in range(share)])  9.75 us
  transfers between devices with their start and end apart: 4, of which 1 were waited for; matrix products, arithmetic and copies ran while one was open for 0% of the time, Pallas kernels for 0%

profile of v6, /device:TPU:1, one launch (start us, length us, event | category | flops | bytes accessed | tf_op | source)
XLA Modules:
  0.0 133.1 jit_solution(5099516366585009889)
XLA Ops:
  1.3 2.0 %start.1 = (bf16[69,16,128]{2,1,0:T(8,128)(2,1)}, bf16[32,4,4,128]{3,2,1,0:T(4,128)(2,1)}) custom-call(bf16[64,64]{1,0:T(8,128)(2,1)} %item_emb.1, bf16[32,64]{1,0:T(8,128)(2,1)} %user_emb.1, s32[1,64]{1,0:T(1,128)} %bitcast.26, s32[1,32]{1,0:T(1,128)} %bitcast.27, s32[1,1,8]{2,1,0:T(1,128)} %rows.1, s32[1,1,8]{2,1,0:T(1,128)} %cols.1, s32[1]{0:T(128)} %bitcast.19.count, ...), custom_call_target="tpu_custom_call" | custom-call | tf_op jit(solution)/shard_map/start/pallas_call | solution.py:305
  3.3 0.0 copy-start
  3.3 5.3 %collective-permute-start.2 = (bf16[69,16,128]{2,1,0:T(8,128)(2,1)}, bf16[69,16,128]{2,1,0:T(8,128)(2,1)S(1)}, u32[]{:S(2)}, u32[]{:S(2)}) collective-permute-start(bf16[69,16,128]{2,1,0:T(8,128)(2,1)} %get-tuple-element.13.p0.payload), channel_id=1, source_target_pairs={{0,3},{1,2},{2,1},{3,0},{4,7},{5,6},{6,5},{7,4},{8,11},{9,10},{10,... | collective-permute-start | bytes 847880 | tf_op jit(solution)/shard_map/payloads_along_x/ppermute | solution.py:333
  8.6 2.4 %collective-permute-start.1 = (bf16[69,16,128]{2,1,0:T(8,128)(2,1)}, bf16[69,16,128]{2,1,0:T(8,128)(2,1)S(1)}, u32[]{:S(2)}, u32[]{:S(2)}) collective-permute-start(bf16[69,16,128]{2,1,0:T(8,128)(2,1)} %get-tuple-element.13.p0.payload), channel_id=1, source_target_pairs={{0,2},{1,3},{2,0},{3,1},{4,6},{5,7},{6,4},{7,5},{8,10},{9,11},{10,... | collective-permute-start | bytes 847880 | tf_op jit(solution)/shard_map/payloads_along_x/ppermute | solution.py:333
  11.1 2.0 %collective-permute-start = (bf16[69,16,128]{2,1,0:T(8,128)(2,1)}, bf16[69,16,128]{2,1,0:T(8,128)(2,1)S(1)}, u32[]{:S(2)}, u32[]{:S(2)}) collective-permute-start(bf16[69,16,128]{2,1,0:T(8,128)(2,1)} %get-tuple-element.13.p0.payload), channel_id=1, source_target_pairs={{0,1},{1,0},{2,3},{3,2},{4,5},{5,4},{6,7},{7,6},{8,9},{9,8},{10,11... | collective-permute-start | bytes 847880 | tf_op jit(solution)/shard_map/payloads_along_x/ppermute | solution.py:333
  13.1 17.1 %all-to-all-start = ((bf16[128,4,128]{2,1,0:T(4,128)(2,1)}), bf16[128,4,128]{2,1,0:T(4,128)(2,1)S(1)}, u32[]{:S(2)}, u32[]{:S(2)}) async-start(bf16[128,4,128]{2,1,0:T(4,128)(2,1)} %bitcast.25), calls=%async_computation | async-start | bytes 262144 | tf_op jit(solution)/shard_map/sent_users_0/all_to_all | solution.py:286
  30.2 0.0 copy-done
  30.2 0.1 slice_bitcast_fusion.3
  30.3 0.1 pad_add_fusion.place
  30.4 0.0 collective-permute-done.2.p3
  30.4 0.1 slice_bitcast_fusion
  30.4 0.0 collective-permute-done.1.p2
  30.4 0.1 slice_bitcast_fusion.1
  30.5 0.0 collective-permute-done.p1
  30.5 0.1 slice_bitcast_fusion.2
  30.6 10.9 %all-to-all-done = bf16[128,4,128]{2,1,0:T(4,128)(2,1)S(1)} async-done(((bf16[128,4,128]{2,1,0:T(4,128)(2,1)}), bf16[128,4,128]{2,1,0:T(4,128)(2,1)S(1)}, u32[]{:S(2)}, u32[]{:S(2)}) %all-to-all-start) | async-done | bytes 131104 | tf_op jit(solution)/shard_map/sent_users_0/all_to_all | solution.py:286
  41.5 1.1 items_1_parts.1
  42.7 34.0 %all-gather = bf16[160,16,128]{2,1,0:T(8,128)(2,1)S(1)} all-gather(bf16[20,16,128]{2,1,0:T(8,128)(2,1)S(1)} %get-tuple-element.15), channel_id=2, replica_groups=mesh['zh'=4,'co'=2,'zl'=4,'y'=8,'x'=4] {'zh','co'}, dimensions={0}, use_global_device_ids=true | all-gather | bytes 737280 | tf_op jit(solution)/shard_map/items_0_and_1/all_gather | solution.py:357
  76.7 1.3 %users_1_and_2_parts.1 = (bf16[32,32,128]{2,1,0:T(8,128)(2,1)S(1)}, f32[4,4,16,128]{3,2,1,0:T(8,128)S(1)}) custom-call(s32[2]{0:T(128)S(1)} %pad_add_fusion.place, s32[4,17]{1,0:T(4,128)S(1)} %maximum_convert_fusion.slots, bf16[69,16,128]{2,1,0:T(8,128)(2,1)S(1)} %copy-done, bf16[69,16,128]{2,1,0:T(8,128)(2,1)S(1)} %collective-permute-done.p1, ...), custom_call_target="tpu_custom_call" | custom-call | tf_op jit(solution)/shard_map/users_1_and_2_parts/pallas_call | solution.py:358
  78.0 14.8 %all_to_all.20.parts = bf16[32,32,128]{2,1,0:T(8,128)(2,1)S(1)} all-to-all(bf16[32,32,128]{2,1,0:T(8,128)(2,1)S(1)} %get-tuple-element.16), channel_id=1, replica_groups=mesh['zh'=4,'co'=2,'zl'=4,'y'=8,'x'=4] {'zl','y'}, dimensions={0} | all-to-all | bytes 524288 | tf_op jit(solution)/shard_map/users_1_and_2/all_to_all | solution.py:286
  92.8 0.1 users_sum.1
  92.9 14.1 %all_to_all.21.users = bf16[32,16,128]{2,1,0:T(8,128)(2,1)S(1)} all-to-all(bf16[32,16,128]{2,1,0:T(8,128)(2,1)S(1)} %get-tuple-element.19), channel_id=1, replica_groups=mesh['zh'=4,'co'=2,'zl'=4,'y'=8,'x'=4] {'zl','y'}, dimensions={0} | all-to-all | bytes 262144 | tf_op jit(solution)/shard_map/sent_users_1/all_to_all | solution.py:286
  107.0 1.1 items_2_parts.1
  108.1 24.1 %all_to_all.22 = bf16[32,3,4,128]{3,2,1,0:T(4,128)(2,1)S(1)} all-to-all(bf16[32,3,4,128]{3,2,1,0:T(4,128)(2,1)S(1)} %bitcast.23), channel_id=1, replica_groups=mesh['zh'=4,'co'=2,'zl'=4,'y'=8,'x'=4] {'x','zh','co'}, dimensions={0} | all-to-all | bytes 196608 | tf_op jit(solution)/shard_map/items_2/all_to_all | solution.py:286
  132.2 0.9 final.1
  (1 shorter events, 0.0 us)
Async XLA Ops:
  3.3 26.9 %copy-start = (bf16[69,16,128]{2,1,0:T(8,128)(2,1)S(1)}, bf16[69,16,128]{2,1,0:T(8,128)(2,1)}, u32[]{:S(2)}) copy-start(bf16[69,16,128]{2,1,0:T(8,128)(2,1)} %get-tuple-element.13.p0.payload) | copy-start | bytes 847876
  3.3 27.1 %collective-permute-start.2 = (bf16[69,16,128]{2,1,0:T(8,128)(2,1)}, bf16[69,16,128]{2,1,0:T(8,128)(2,1)S(1)}, u32[]{:S(2)}, u32[]{:S(2)}) collective-permute-start(bf16[69,16,128]{2,1,0:T(8,128)(2,1)} %get-tuple-element.13.p0.payload), channel_id=1, source_target_pairs={{0,3},{1,2},{2,1},{3,0},{4,7},{5,6},{6,5},{7,4},{8,11},{9,10},{10,... | collective-permute-start | bytes 847880 | tf_op jit(solution)/shard_map/payloads_along_x/ppermute | solution.py:333
  8.6 21.8 %collective-permute-start.1 = (bf16[69,16,128]{2,1,0:T(8,128)(2,1)}, bf16[69,16,128]{2,1,0:T(8,128)(2,1)S(1)}, u32[]{:S(2)}, u32[]{:S(2)}) collective-permute-start(bf16[69,16,128]{2,1,0:T(8,128)(2,1)} %get-tuple-element.13.p0.payload), channel_id=1, source_target_pairs={{0,2},{1,3},{2,0},{3,1},{4,6},{5,7},{6,4},{7,5},{8,10},{9,11},{10,... | collective-permute-start | bytes 847880 | tf_op jit(solution)/shard_map/payloads_along_x/ppermute | solution.py:333
  11.1 19.5 %collective-permute-start = (bf16[69,16,128]{2,1,0:T(8,128)(2,1)}, bf16[69,16,128]{2,1,0:T(8,128)(2,1)S(1)}, u32[]{:S(2)}, u32[]{:S(2)}) collective-permute-start(bf16[69,16,128]{2,1,0:T(8,128)(2,1)} %get-tuple-element.13.p0.payload), channel_id=1, source_target_pairs={{0,1},{1,0},{2,3},{3,2},{4,5},{5,4},{6,7},{7,6},{8,9},{9,8},{10,11... | collective-permute-start | bytes 847880 | tf_op jit(solution)/shard_map/payloads_along_x/ppermute | solution.py:333
  13.1 28.5 %all-to-all-start = ((bf16[128,4,128]{2,1,0:T(4,128)(2,1)}), bf16[128,4,128]{2,1,0:T(4,128)(2,1)S(1)}, u32[]{:S(2)}, u32[]{:S(2)}) async-start(bf16[128,4,128]{2,1,0:T(4,128)(2,1)} %bitcast.25), calls=%async_computation | async-start | bytes 262144 | tf_op jit(solution)/shard_map/sent_users_0/all_to_all | solution.py:286

commit v7 on v5

--- a/solution.py
+++ b/solution.py
@@ -172,6 +172,7 @@
         for col in range(tile_cols):
             out[x * tile_cols + col] = acc[x, col].astype(BF16)
     first_block = share * tile_cols
+    degrees = []
     for pair in range(share // 2):
         first, degree = (
             jnp.concatenate(
@@ -180,7 +181,8 @@
             for part in range(2)
         )
         out[first_block + pair] = (lax.rsqrt(degree) * first).astype(BF16)
-        out[first_block + share // 2 + pair] = degree.astype(BF16)
+        degrees.append(degree[: step // 2])
+    out[first_block + share // 2] = jnp.concatenate(degrees, axis=0).astype(BF16)
 
 
 def users_kernel(place, slots, p0, p1, p2, p3, gathered, out, item_sum, acc, sent):
@@ -203,7 +205,18 @@
             for part in range(1, n_row):
                 total = total + gathered[part, at].astype(F32)
             item_sum[x, col] = total
-            scale = lax.rsqrt(of_tile(base + share // 2, x, col))
+            line, side = (x // 2) * (step // 2), (x % 2) * half
+            scale = lax.rsqrt(
+                jnp.concatenate(
+                    [
+                        gathered[2 * col + k, base + share // 2].astype(F32)[
+                            line : line + 1, side : side + half
+                        ]
+                        for k in range(2)
+                    ],
+                    axis=1,
+                )
+            )
             sent[x, col, :step] = of_tile(base, x, col).astype(BF16)
             sent[x, col, step:] = (scale * (scale * total)).astype(BF16)
     acc[...] = jnp.zeros_like(acc)
@@ -340,7 +353,7 @@
     ).astype(jnp.int32)
     slotted = [SMEM] * 2 + [VMEM] * share
     slot_args = (place, slots, *payloads)
-    blocks = share * tile_cols + share
+    blocks = share * tile_cols + share // 2 + 1
     first_shape = message.shape
     message, user_zero, user_scale = call(
         items_one_kernel,

time: 133 us -> 133 us (level)
  no operation moved by 1% of the time
where the time goes in v7:
time: 133 us; the launch traced here: 132 us
  blocking collectives  86.5 us (65%)
  starting transfers between devices  26.6 us (20%)
  waiting for transfers between devices  11 us (8%)
  Pallas kernels  6.45 us (5%)
  between operations  1.37 us (1%)
    all_to_all x3, blocking collectives, exchange(): return lax.all_to_all(values, axes, split_axis=0, concat_axis=0, tiled=True)  52.8 us
    all_gather x1, blocking collectives, per_device(): gathered = lax.all_gather(message, ROW, axis=0)  33.7 us
    all_to_all x1, starting transfers between devices, exchange(): return lax.all_to_all(values, axes, split_axis=0, concat_axis=0, tiled=True)  16.3 us
    all_to_all x1, waiting for transfers between devices, exchange(): return lax.all_to_all(values, axes, split_axis=0, concat_axis=0, tiled=True)  10.9 us
    ppermute x3, starting transfers between devices, per_device(): lax.ppermute(payload, 'x', [(x, (x + away) % share) for x in range(share)])  10.3 us
  transfers between devices with their start and end apart: 4, of which 1 were waited for; matrix products, arithmetic and copies ran while one was open for 0% of the time, Pallas kernels for 0%

profile of v7, /device:TPU:1, one launch (start us, length us, event | category | flops | bytes accessed | tf_op | source)
XLA Modules:
  0.0 132.2 jit_solution(6008188121181896577)
XLA Ops:
  1.3 2.0 %start.1 = (bf16[69,16,128]{2,1,0:T(8,128)(2,1)}, bf16[32,4,4,128]{3,2,1,0:T(4,128)(2,1)}) custom-call(bf16[64,64]{1,0:T(8,128)(2,1)} %item_emb.1, bf16[32,64]{1,0:T(8,128)(2,1)} %user_emb.1, s32[1,64]{1,0:T(1,128)} %bitcast.26, s32[1,32]{1,0:T(1,128)} %bitcast.27, s32[1,1,8]{2,1,0:T(1,128)} %rows.1, s32[1,1,8]{2,1,0:T(1,128)} %cols.1, s32[1]{0:T(128)} %bitcast.19.count, ...), custom_call_target="tpu_custom_call" | custom-call | tf_op jit(solution)/shard_map/start/pallas_call | solution.py:318
  3.3 0.0 copy-start
  3.3 5.3 %collective-permute-start.2 = (bf16[69,16,128]{2,1,0:T(8,128)(2,1)}, bf16[69,16,128]{2,1,0:T(8,128)(2,1)S(1)}, u32[]{:S(2)}, u32[]{:S(2)}) collective-permute-start(bf16[69,16,128]{2,1,0:T(8,128)(2,1)} %get-tuple-element.13.p0.payload), channel_id=1, source_target_pairs={{0,3},{1,0},{2,1},{3,2},{4,7},{5,4},{6,5},{7,6},{8,11},{9,8},{10,9... | collective-permute-start | bytes 847880 | tf_op jit(solution)/shard_map/payloads_along_x/ppermute | solution.py:346
  8.6 2.4 %collective-permute-start.1 = (bf16[69,16,128]{2,1,0:T(8,128)(2,1)}, bf16[69,16,128]{2,1,0:T(8,128)(2,1)S(1)}, u32[]{:S(2)}, u32[]{:S(2)}) collective-permute-start(bf16[69,16,128]{2,1,0:T(8,128)(2,1)} %get-tuple-element.13.p0.payload), channel_id=1, source_target_pairs={{0,2},{1,3},{2,0},{3,1},{4,6},{5,7},{6,4},{7,5},{8,10},{9,11},{10,... | collective-permute-start | bytes 847880 | tf_op jit(solution)/shard_map/payloads_along_x/ppermute | solution.py:346
  11.1 2.5 %collective-permute-start = (bf16[69,16,128]{2,1,0:T(8,128)(2,1)}, bf16[69,16,128]{2,1,0:T(8,128)(2,1)S(1)}, u32[]{:S(2)}, u32[]{:S(2)}) collective-permute-start(bf16[69,16,128]{2,1,0:T(8,128)(2,1)} %get-tuple-element.13.p0.payload), channel_id=1, source_target_pairs={{0,1},{1,2},{2,3},{3,0},{4,5},{5,6},{6,7},{7,4},{8,9},{9,10},{10,1... | collective-permute-start | bytes 847880 | tf_op jit(solution)/shard_map/payloads_along_x/ppermute | solution.py:346
  13.6 16.3 %all-to-all-start = ((bf16[128,4,128]{2,1,0:T(4,128)(2,1)}), bf16[128,4,128]{2,1,0:T(4,128)(2,1)S(1)}, u32[]{:S(2)}, u32[]{:S(2)}) async-start(bf16[128,4,128]{2,1,0:T(4,128)(2,1)} %bitcast.25), calls=%async_computation | async-start | bytes 262144 | tf_op jit(solution)/shard_map/sent_users_0/all_to_all | solution.py:299
  29.9 0.0 copy-done
  29.9 0.1 slice_bitcast_fusion.3
  30.0 0.1 pad_add_fusion.place
  30.0 0.0 collective-permute-done.2.p3
  30.0 0.1 slice_bitcast_fusion
  30.1 0.0 collective-permute-done.1.p2
  30.1 0.1 slice_bitcast_fusion.1
  30.2 0.0 collective-permute-done.p1
  30.2 0.1 slice_bitcast_fusion.2
  30.3 10.9 %all-to-all-done = bf16[128,4,128]{2,1,0:T(4,128)(2,1)S(1)} async-done(((bf16[128,4,128]{2,1,0:T(4,128)(2,1)}), bf16[128,4,128]{2,1,0:T(4,128)(2,1)S(1)}, u32[]{:S(2)}, u32[]{:S(2)}) %all-to-all-start) | async-done | bytes 131104 | tf_op jit(solution)/shard_map/sent_users_0/all_to_all | solution.py:299
  41.2 1.1 items_1_parts.1
  42.4 33.7 %all-gather = bf16[152,16,128]{2,1,0:T(8,128)(2,1)S(1)} all-gather(bf16[19,16,128]{2,1,0:T(8,128)(2,1)S(1)} %get-tuple-element.15), channel_id=2, replica_groups=mesh['zh'=4,'co'=2,'zl'=4,'y'=8,'x'=4] {'zh','co'}, dimensions={0}, use_global_device_ids=true | all-gather | bytes 700416 | tf_op jit(solution)/shard_map/items_0_and_1/all_gather | solution.py:370
  76.0 1.3 %users_1_and_2_parts.1 = (bf16[32,32,128]{2,1,0:T(8,128)(2,1)S(1)}, f32[4,4,16,128]{3,2,1,0:T(8,128)S(1)}) custom-call(s32[2]{0:T(128)S(1)} %pad_add_fusion.place, s32[4,17]{1,0:T(4,128)S(1)} %maximum_convert_fusion.slots, bf16[69,16,128]{2,1,0:T(8,128)(2,1)S(1)} %copy-done, bf16[69,16,128]{2,1,0:T(8,128)(2,1)S(1)} %collective-permute-done.p1, ...), custom_call_target="tpu_custom_call" | custom-call | tf_op jit(solution)/shard_map/users_1_and_2_parts/pallas_call | solution.py:371
  77.4 14.8 %all_to_all.20.parts = bf16[32,32,128]{2,1,0:T(8,128)(2,1)S(1)} all-to-all(bf16[32,32,128]{2,1,0:T(8,128)(2,1)S(1)} %get-tuple-element.16), channel_id=1, replica_groups=mesh['zh'=4,'co'=2,'zl'=4,'y'=8,'x'=4] {'zl','y'}, dimensions={0} | all-to-all | bytes 524288 | tf_op jit(solution)/shard_map/users_1_and_2/all_to_all | solution.py:299
  92.2 0.1 users_sum.1
  92.2 14.1 %all_to_all.21.users = bf16[32,16,128]{2,1,0:T(8,128)(2,1)S(1)} all-to-all(bf16[32,16,128]{2,1,0:T(8,128)(2,1)S(1)} %get-tuple-element.19), channel_id=1, replica_groups=mesh['zh'=4,'co'=2,'zl'=4,'y'=8,'x'=4] {'zl','y'}, dimensions={0} | all-to-all | bytes 262144 | tf_op jit(solution)/shard_map/sent_users_1/all_to_all | solution.py:299
  106.4 1.1 items_2_parts.1
  107.5 23.9 %all_to_all.22 = bf16[32,3,4,128]{3,2,1,0:T(4,128)(2,1)S(1)} all-to-all(bf16[32,3,4,128]{3,2,1,0:T(4,128)(2,1)S(1)} %bitcast.23), channel_id=1, replica_groups=mesh['zh'=4,'co'=2,'zl'=4,'y'=8,'x'=4] {'zh','co','x'}, dimensions={0} | all-to-all | bytes 196608 | tf_op jit(solution)/shard_map/items_2/all_to_all | solution.py:299
  131.3 0.9 final.1
  (1 shorter events, 0.0 us)
Async XLA Ops:
  3.3 26.6 %copy-start = (bf16[69,16,128]{2,1,0:T(8,128)(2,1)S(1)}, bf16[69,16,128]{2,1,0:T(8,128)(2,1)}, u32[]{:S(2)}) copy-start(bf16[69,16,128]{2,1,0:T(8,128)(2,1)} %get-tuple-element.13.p0.payload) | copy-start | bytes 847876
  3.3 26.8 %collective-permute-start.2 = (bf16[69,16,128]{2,1,0:T(8,128)(2,1)}, bf16[69,16,128]{2,1,0:T(8,128)(2,1)S(1)}, u32[]{:S(2)}, u32[]{:S(2)}) collective-permute-start(bf16[69,16,128]{2,1,0:T(8,128)(2,1)} %get-tuple-element.13.p0.payload), channel_id=1, source_target_pairs={{0,3},{1,0},{2,1},{3,2},{4,7},{5,4},{6,5},{7,6},{8,11},{9,8},{10,9... | collective-permute-start | bytes 847880 | tf_op jit(solution)/shard_map/payloads_along_x/ppermute | solution.py:346
  8.6 21.5 %collective-permute-start.1 = (bf16[69,16,128]{2,1,0:T(8,128)(2,1)}, bf16[69,16,128]{2,1,0:T(8,128)(2,1)S(1)}, u32[]{:S(2)}, u32[]{:S(2)}) collective-permute-start(bf16[69,16,128]{2,1,0:T(8,128)(2,1)} %get-tuple-element.13.p0.payload), channel_id=1, source_target_pairs={{0,2},{1,3},{2,0},{3,1},{4,6},{5,7},{6,4},{7,5},{8,10},{9,11},{10,... | collective-permute-start | bytes 847880 | tf_op jit(solution)/shard_map/payloads_along_x/ppermute | solution.py:346
  11.1 19.1 %collective-permute-start = (bf16[69,16,128]{2,1,0:T(8,128)(2,1)}, bf16[69,16,128]{2,1,0:T(8,128)(2,1)S(1)}, u32[]{:S(2)}, u32[]{:S(2)}) collective-permute-start(bf16[69,16,128]{2,1,0:T(8,128)(2,1)} %get-tuple-element.13.p0.payload), channel_id=1, source_target_pairs={{0,1},{1,2},{2,3},{3,0},{4,5},{5,6},{6,7},{7,4},{8,9},{9,10},{10,1... | collective-permute-start | bytes 847880 | tf_op jit(solution)/shard_map/payloads_along_x/ppermute | solution.py:346
  13.6 27.6 %all-to-all-start = ((bf16[128,4,128]{2,1,0:T(4,128)(2,1)}), bf16[128,4,128]{2,1,0:T(4,128)(2,1)S(1)}, u32[]{:S(2)}, u32[]{:S(2)}) async-start(bf16[128,4,128]{2,1,0:T(4,128)(2,1)} %bitcast.25), calls=%async_computation | async-start | bytes 262144 | tf_op jit(solution)/shard_map/sent_users_0/all_to_all | solution.py:299
